TPU v7x, 32 devices: a whole 2x2x4 slice. The times are simulated.
32 devices in a mesh: row: 4 (over y, x), col: 8 (over z, core).
Axes of the slice: x: 2, y: 2, z: 4, core: 2. Of those that a mesh axis runs over, the one named last changes fastest.
Arguments:
- latent: bfloat16 [128, 40960], P('row', 'col'), may hold values from -6 to 6
- tile_reach: int32 [4, 8, 4], replicated, may hold values from 1 to 4
- first_weight: bfloat16 [3, 3, 320, 320], replicated, may hold values from -0.109375 to 0.109375
- first_bias: float32 [320], replicated, may hold values from -3 to 3
- second_weight: bfloat16 [3, 3, 320, 320], replicated, may hold values from -0.109375 to 0.109375
- second_bias: float32 [320], replicated, may hold values from -3 to 3
- proj_weight: bfloat16 [320, 512], replicated, may hold values from -0.3125 to 0.3125
- upper_weight: bfloat16 [3, 3, 512, 512], replicated, may hold values from -0.09375 to 0.09375
- upper_bias: float32 [512], replicated, may hold values from -3 to 3
- lower_weight: bfloat16 [3, 3, 512, 512], replicated, may hold values from -0.09375 to 0.09375
- lower_bias: float32 [512], replicated, may hold values from -3 to 3
Outputs:
- decoded: bfloat16 [256, 256, 512], P(('row', 'col'))
All inputs are finite; a program needn't handle non-finite values.
Results may differ from a plain program's by a relative error of at most 0.0065.
Values may be sent and summed in bfloat16 or wider, within the bound.
No kernel may reach another device: no remote copies, remote signals or barrier semaphores. Data moves between devices by JAX's collectives and lax.ppermute only.
A program may use at most 64 MiB of HBM per device.

v0:
```python
import jax
import jax.numpy as jnp
from jax import lax
from jax.experimental import pallas as pl
from jax.experimental.pallas import tpu as pltpu
from jax.sharding import PartitionSpec as P

BF = jnp.bfloat16
F32 = jnp.float32
MARGIN = 4
HALO = 3
VMEM_LIMIT = 62 * 1024 * 1024


def silu(v):
    return v / (1.0 + jnp.exp(-v))


def tap_kernel(w_ref, main_ref, rest_ref):
    chans = w_ref.shape[2]
    main = chans // 128 * 128
    rest = chans - main
    depth = main_ref.shape[0] // 3
    main_ref[...] = jnp.zeros_like(main_ref)
    rest_ref[...] = jnp.zeros_like(rest_ref)
    for dy in range(3):
        for dx in range(3):
            main_ref[dy * depth + dx * main : dy * depth + dx * main + main, :] = w_ref[dy, dx, :main, :main]
            at = 3 * main + dx * rest
            main_ref[dy * depth + at : dy * depth + at + rest, :] = w_ref[dy, dx, main:, :main]
    for dx in range(3):
        for lo, n, at in ((0, main, dx * main), (main, rest, 3 * main + dx * rest)):
            tails = [w_ref[dy, dx, lo : lo + n, main:].astype(F32) for dy in range(3)]
            rest_ref[at : at + n, :128] = jnp.concatenate(tails[:2], axis=1).astype(BF)
            rest_ref[at : at + n, 128 : 128 + rest] = tails[2].astype(BF)


def setup_kernel(w1_ref, w2_ref, m1_ref, r1_ref, m2_ref, r2_ref):
    tap_kernel(w1_ref, m1_ref, r1_ref)
    tap_kernel(w2_ref, m2_ref, r2_ref)


def setup_call(w1, w2):
    chans = w1.shape[2]
    main = chans // 128 * 128
    rest = chans - main
    assert 2 * rest == 128
    depth = 3 * main + 4 * rest
    taps = [jax.ShapeDtypeStruct((3 * depth, main), BF), jax.ShapeDtypeStruct((depth, 256), BF)]
    return pl.pallas_call(
        setup_kernel,
        out_shape=taps + taps,
        compiler_params=pltpu.CompilerParams(vmem_limit_bytes=VMEM_LIMIT),
        cost_estimate=pl.CostEstimate(flops=0, bytes_accessed=8 << 20, transcendentals=0),
    )(w1, w2)


def put_cells(main_ref, rest_ref, r, v, main):
    span = v.shape[0]
    main_ref[r, pl.ds(1, span)] = v[:, :, :main].astype(BF)
    rest = v[:, :, main:]
    none = jnp.zeros((1,) + rest.shape[1:], F32)
    before = jnp.concatenate([none, rest[:-1]], axis=0)
    after = jnp.concatenate([rest[1:], none], axis=0)
    rest_ref[r, :, :, :128] = (before + pltpu.roll(rest, 64, 2)).astype(BF)
    rest_ref[r, :, :, 128:] = after.astype(BF)


def conv_group(main_ref, rest_ref, w_main, w_rest, start, rows):
    span, slots = rest_ref.shape[1:3]
    main = main_ref.shape[3]
    size = rows * span * slots
    parts = []
    for dy in range(3):
        for dx in range(3):
            parts.append(main_ref[pl.ds(start + dy, rows), pl.ds(dx, span)].reshape(size, main))
        parts.append(rest_ref[pl.ds(start + dy, rows)].reshape(size, 256))
    big = jnp.dot(jnp.concatenate(parts, axis=1), w_main[...], preferred_element_type=F32)
    size = (rows + 2) * span * slots
    parts = [main_ref[pl.ds(start, rows + 2), pl.ds(dx, span)].reshape(size, main) for dx in range(3)]
    parts.append(rest_ref[pl.ds(start, rows + 2)].reshape(size, 256))
    part = jnp.dot(jnp.concatenate(parts, axis=1), w_rest[...], preferred_element_type=F32)
    part = part.reshape(rows + 2, span, slots, 256)
    rest = part[:-2, :, :, :128] + pltpu.roll(part[1:-1, :, :, :128], 64, 3) + part[2:, :, :, 128:]
    return big.reshape(rows, span, slots, main), rest


def tile_body(geom, chans, tall, bounds_ref, m1, r1, b1_ref, m2, r2, b2_ref, canvas, xm, xr, am, ar, cells_ref, beside):
    n_row, n_col, tile_rows, tile_cols, own = geom
    slots = 2 * n_col
    span = tile_cols + 2 * MARGIN
    main = chans // 128 * 128
    lanes = main + 128
    rows_x = own + 2 * HALO
    width = n_col * tile_cols
    live = (lax.broadcasted_iota(jnp.int32, (1, 1, 128), 2) < chans - main).astype(F32)
    cell = lax.broadcasted_iota(jnp.int32, (span, slots, 128), 0)
    cols_ok = ((cell >= bounds_ref[2]) & (cell < bounds_ref[3])).astype(F32)
    xm[...] = jnp.zeros_like(xm)
    am[...] = jnp.zeros_like(am)

    def mask_of(r):
        row = jnp.zeros((slots, 128), jnp.int32) + r
        rows_ok = ((row >= bounds_ref[0]) & (row < bounds_ref[1])).astype(F32)
        return cols_ok * rows_ok

    def wide(m):
        return jnp.concatenate([m] * (lanes // 128), axis=2)

    r = 0
    for piece in tall:
        for k in range(piece.shape[0]):
            cols = []
            for c in range(tile_cols):
                lo = c * chans
                off = lo % 128
                v = piece[k, :, lo - off : lo - off + lanes].astype(F32)
                if off:
                    v = pltpu.roll(v, lanes - off, 1)
                cols.append(v)
            cells_ref[...] = jnp.stack(cols, axis=0)
            v = cells_ref[...]
            v = jnp.concatenate([v[:, :, :main], v[:, :, main:] * live], axis=2)
            v = jnp.concatenate(
                [pltpu.roll(v[-MARGIN:], 1, 1), v, pltpu.roll(v[:MARGIN], n_col - 1, 1)], axis=0)
            v = jnp.concatenate([v, v], axis=1)
            put_cells(xm, xr, r, v * wide(mask_of(r)), main)
            r += 1

    group1 = (rows_x - 2) // 2
    def first(g, carry):
        beside[0](g)
        big, rest = conv_group(xm, xr, m1, r1, g * group1, group1)
        for i in range(group1):
            a = g * group1 + i
            v = jnp.concatenate([big[i], rest[i] * live], axis=2) + b1_ref[...]
            put_cells(am, ar, a, silu(v) * wide(mask_of(a + 1)), main)
        return carry
    lax.fori_loop(0, 2, first, 0)

    group2 = (rows_x - 4) // 2
    def second(g, carry):
        beside[1](g)
        big, rest = conv_group(am, ar, m2, r2, g * group2, group2)
        for i in range(group2):
            a = g * group2 + i
            v = jnp.concatenate([big[i], rest[i] * live], axis=2) + b2_ref[...]
            x_rest = pltpu.roll(xr[a + 2, :, :, :128].astype(F32), 64, 2) * live
            x = jnp.concatenate([xm[a + 2, pl.ds(1, span)].astype(F32), x_rest], axis=2)
            mask = mask_of(a + 2)
            y = ((v + x) * wide(mask)).astype(BF).astype(F32)

            def fold(u):
                u = u[:, :n_col] + u[:, n_col:]
                mid = u[MARGIN:-MARGIN]
                return jnp.concatenate(
                    [
                        mid[:MARGIN] + pltpu.roll(u[-MARGIN:], 1, 1),
                        mid[MARGIN:-MARGIN],
                        mid[-MARGIN:] + pltpu.roll(u[:MARGIN], n_col - 1, 1),
                    ],
                    axis=0,
                )

            count = fold(mask)
            blend = fold(y) * wide(jnp.where(count > 0, 1.0 / jnp.maximum(count, 1.0), 0.0))
            for c in range(tile_cols):
                for lane in range(lanes // 128):
                    canvas[lane, pl.ds(a * width + c, n_col, stride=tile_cols), :] = blend[c, :, lane * 128 : lane * 128 + 128]
        return carry
    lax.fori_loop(0, 2, second, 0)


def tile_scratch(geom, chans):
    n_row, n_col, tile_rows, tile_cols, own = geom
    slots = 2 * n_col
    span = tile_cols + 2 * MARGIN
    main = chans // 128 * 128
    rows_x = own + 2 * HALO
    return [
        pltpu.VMEM((main // 128 + 1, (own + 2) * n_col * tile_cols, 128), F32),
        pltpu.VMEM((rows_x, span + 2, slots, main), BF),
        pltpu.VMEM((rows_x, span, slots, 256), BF),
        pltpu.VMEM((rows_x - 2, span + 2, slots, main), BF),
        pltpu.VMEM((rows_x - 2, span, slots, 256), BF),
        pltpu.VMEM((tile_cols, n_col, main + 128), F32),
    ]


def phase_part(w, out, k0, kn):
    ks = pl.ds(k0, kn)
    depth = w.shape[1]
    x = [[w[3 * dy + dx, ks, :].astype(F32) for dx in range(3)] for dy in range(3)]
    rowed = (
        (x[0], [a + b for a, b in zip(x[1], x[2])]),
        ([a + b for a, b in zip(x[0], x[1])], x[2]),
    )
    for p in range(2):
        for tap in range(2):
            u = rowed[p][tap]
            at = 2 * tap * depth + k0
            out[0, p, pl.ds(at, kn), :] = u[0].astype(BF)
            out[0, p, pl.ds(at + depth, kn), :] = (u[1] + u[2]).astype(BF)
            out[1, p, pl.ds(at, kn), :] = (u[0] + u[1]).astype(BF)
            out[1, p, pl.ds(at + depth, kn), :] = u[2].astype(BF)


def pair_part(w, out, k0, kn):
    ks = pl.ds(k0, kn)
    for dy in range(3):
        ends = 0.5 * (w[3 * dy, ks, :].astype(F32) + w[3 * dy + 2, ks, :].astype(F32))
        mid = 0.5 * w[3 * dy + 1, ks, :].astype(F32)
        w[3 * dy + 1, ks, :] = (ends + mid).astype(BF)
        out[dy, ks, :] = (ends - mid).astype(BF)


def decoder_body(
    keep, canvas, proj_ref, ub_ref, lb_ref, out_ref, left, hid, right, comps, edge, zipped,
    upper_v, lower_raw, pair_v,
):
    rows, width, dc = hid.shape
    steps = rows - 1
    own = rows - 2
    chans = proj_ref.shape[0]
    main = chans // 128 * 128

    edge[...] = jnp.zeros_like(edge)

    def hidden_row(r, carry):
        at = pl.ds(pl.multiple_of(r * width, width), width)
        x = jnp.concatenate([canvas[lane, at, :] for lane in range(main // 128)], axis=1).astype(BF)
        rest = canvas[main // 128, at, :].astype(BF)[:, : chans - main]
        h = jnp.dot(x, proj_ref[:main, :], preferred_element_type=F32)
        h = h + jnp.dot(rest, proj_ref[main:, :], preferred_element_type=F32)
        h = h.astype(BF)
        hid[r] = h
        edge[0, pl.ds(8, width), :] = h.astype(F32)
        left[r] = edge[0, pl.ds(7, width), :].astype(BF)
        right[r] = edge[0, pl.ds(9, width), :].astype(BF)
        return carry

    lax.fori_loop(0, rows, hidden_row, 0)

    def up_step(p, carry):
        acts = []
        for side, srcs in ((0, (left, hid)), (1, (hid, right))):
            lhs = jnp.concatenate(
                [src[pl.ds(i, steps)].reshape(steps * width, dc) for i in range(2) for src in srcs], axis=1
            )
            v = jnp.dot(lhs, upper_v[side, p], preferred_element_type=F32)
            acts.append(silu(v + ub_ref[...]).reshape(steps, width, dc))
        for k in range(steps):
            scale = 1.0
            if k == 0:
                scale = jnp.where(p == 1, keep[0], 1.0)
            if k == steps - 1:
                scale = jnp.where(p == 0, keep[1], 1.0)
            e = (acts[0][k] * scale).astype(BF).astype(F32)
            o = (acts[1][k] * scale).astype(BF).astype(F32)
            edge[0, pl.ds(8, width), :] = o
            edge[1, pl.ds(8, width), :] = e
            at = 2 * k + 1 - p
            comps[0, at] = (edge[0, pl.ds(7, width), :] - o).astype(BF)
            comps[1, at] = (e + o).astype(BF)
            comps[2, at] = (o - e).astype(BF)
            comps[3, at] = (e - edge[1, pl.ds(9, width), :]).astype(BF)
        return carry

    lax.fori_loop(0, 2, up_step, 0)

    group = max(own, 1)

    def low_step(n, carry):
        start = n * group
        prods = []
        for i in range(4):
            total = None
            for dy in range(3):
                lhs = comps[i, pl.ds(start + dy, group)].reshape(group * width, dc)
                rhs = pair_v[dy] if i == 2 else lower_raw[3 * dy + (0, 1, 0, 2)[i]]
                v = jnp.dot(lhs, rhs, preferred_element_type=F32)
                total = v if total is None else total + v
            prods.append(total)
        both = (prods[0] + prods[1] + prods[2], prods[1] - prods[2] - prods[3])
        for g in range(group):
            base = hid[1 + lax.div(start + g, 2)].astype(F32) + lb_ref[...]
            for side in range(2):
                v = both[side][g * width : (g + 1) * width] + base
                for lane in range(dc // 128):
                    zipped[lane, pl.ds(g * 2 * width + side, width, stride=2), :] = v[:, lane * 128 : lane * 128 + 128]
            for lane in range(dc // 128):
                out_ref[start + g, :, pl.ds(lane * 128, 128)] = zipped[lane, pl.ds(g * 2 * width, 2 * width), :].astype(BF)
        return carry

    lax.fori_loop(0, 2 * own // group, low_step, 0)


def main_kernel(
    geom, chans, n_tall, ids_ref, bounds_ref, m1, r1, m2, r2, bias_ref, proj_ref, upper_ref, lower_ref, *refs
):
    n_row, n_col, tile_rows, tile_cols, own = geom
    tall, refs = refs[:n_tall], refs[n_tall:]
    (out_ref, canvas, xm, xr, am, ar, cells_ref, left, hid, right, comps, edge, zipped,
     upper_raw, upper_v, lower_raw, pair_v, sems) = refs
    upper_copy = pltpu.make_async_copy(upper_ref, upper_raw, sems.at[0])
    lower_copy = pltpu.make_async_copy(lower_ref, lower_raw, sems.at[1])
    upper_copy.start()
    lower_copy.start()
    first_row = ids_ref[0] * tile_rows + ids_ref[1] * own
    keep = (
        jnp.where(first_row > 0, 1.0, 0.0),
        jnp.where(first_row + own < n_row * tile_rows, 1.0, 0.0),
    )
    lanes = chans // 128 * 128 + 128
    bias1, bias2 = bias_ref.at[pl.ds(0, 1), pl.ds(0, lanes)], bias_ref.at[pl.ds(1, 1), pl.ds(0, lanes)]
    part = upper_raw.shape[1] // 4

    def beside_first(g):
        @pl.when(g == 0)
        def _():
            upper_copy.wait()
        phase_part(upper_raw, upper_v, pl.multiple_of(g * part, part), part)

    def beside_second(g):
        @pl.when(g == 0)
        def _():
            lower_copy.wait()
        phase_part(upper_raw, upper_v, pl.multiple_of((g + 2) * part, part), part)
        pair_part(lower_raw, pair_v, pl.multiple_of(2 * g * part, 2 * part), 2 * part)

    tile_body(
        geom, chans, tall, bounds_ref, m1, r1, bias1, m2, r2, bias2, canvas, xm, xr, am, ar, cells_ref,
        (beside_first, beside_second),
    )
    decoder_body(
        keep, canvas, proj_ref, bias_ref.at[pl.ds(2, 1)], bias_ref.at[pl.ds(3, 1)], out_ref,
        left, hid, right, comps, edge, zipped, upper_v, lower_raw, pair_v,
    )


def main_call(geom, ids, tall, bounds, m1, r1, m2, r2, biases, proj, upper, lower, chans):
    n_row, n_col, tile_rows, tile_cols, own = geom
    width = n_col * tile_cols
    rows = own + 2
    dc = proj.shape[1]
    vm = pl.BlockSpec(memory_space=pltpu.VMEM)
    anyspace = pl.BlockSpec(memory_space=pl.ANY)

    def kernel(*refs):
        main_kernel(geom, chans, len(tall), *refs)

    return pl.pallas_call(
        kernel,
        out_shape=jax.ShapeDtypeStruct((2 * own, 2 * width, dc), BF),
        in_specs=[pl.BlockSpec(memory_space=pltpu.SMEM)] + [vm] * 7 + [anyspace] * 2 + [vm] * len(tall),
        out_specs=vm,
        scratch_shapes=tile_scratch(geom, chans)
        + [
            pltpu.VMEM((rows, width, dc), BF),
            pltpu.VMEM((rows, width, dc), BF),
            pltpu.VMEM((rows, width, dc), BF),
            pltpu.VMEM((4, 2 * own + 2, width, dc), BF),
            pltpu.VMEM((2, width + 16, dc), F32),
            pltpu.VMEM((dc // 128, 2 * own * width, 128), F32),
            pltpu.VMEM(upper.shape, BF),
            pltpu.VMEM((2, 2, 4 * dc, dc), BF),
            pltpu.VMEM(lower.shape, BF),
            pltpu.VMEM((3, dc, dc), BF),
            pltpu.SemaphoreType.DMA((2,)),
        ],
        compiler_params=pltpu.CompilerParams(vmem_limit_bytes=VMEM_LIMIT),
        cost_estimate=pl.CostEstimate(flops=25_000_000_000, bytes_accessed=20 << 20, transcendentals=0),
    )(ids, bounds, m1, r1, m2, r2, biases, proj, upper, lower, *tall)


def tile_bounds(tile_reach, row_id, col_id, n_row, n_col, tile_rows, tile_cols, own):
    first_row = row_id * tile_rows + col_id * own - HALO
    other = jnp.where(col_id < n_col // 2, row_id - 1, row_id + 1)
    bands = jnp.stack([row_id, other])
    reach = tile_reach[jnp.clip(bands, 0, n_row - 1)]
    bands = bands[:, None]
    tiles = jnp.arange(n_col, dtype=jnp.int32)[None, :]
    row_lo = jnp.maximum(bands * tile_rows - reach[:, :, 0], 0) - first_row
    row_hi = jnp.minimum((bands + 1) * tile_rows + reach[:, :, 1], n_row * tile_rows) - first_row
    row_hi = jnp.where((bands >= 0) & (bands < n_row), row_hi, 0)
    col_lo = jnp.where(tiles > 0, MARGIN - reach[:, :, 2], MARGIN)
    col_hi = jnp.where(tiles < n_col - 1, MARGIN + tile_cols + reach[:, :, 3], MARGIN + tile_cols)
    return jnp.stack([row_lo, row_hi, col_lo, col_hi]).reshape(4, 2 * n_col).astype(jnp.int32)


def halo_rows(rows, n_all):
    own = rows.shape[0]
    above, below = [], []
    left, hop = HALO, 1
    while left > 0:
        take = min(own, left)
        above.insert(0, lax.ppermute(rows[own - take :], ("row", "col"), [(i, i + hop) for i in range(n_all - hop)]))
        below.append(lax.ppermute(rows[:take], ("row", "col"), [(i + hop, i) for i in range(n_all - hop)]))
        left -= take
        hop += 1
    return above, below


def on_device(
    latent, tile_reach, first_weight, first_bias, second_weight, second_bias, proj_weight,
    upper_weight, upper_bias, lower_weight, lower_bias,
):
    chans = first_weight.shape[2]
    dc = proj_weight.shape[1]
    tile_rows = latent.shape[0]
    tile_cols = latent.shape[1] // chans
    n_row = lax.axis_size("row")
    n_col = lax.axis_size("col")
    row_id = lax.axis_index("row")
    col_id = lax.axis_index("col")
    own = tile_rows // n_col
    geom = (n_row, n_col, tile_rows, tile_cols, own)

    moved = lax.all_to_all(
        latent.reshape(n_col, own, tile_cols * chans), "col", split_axis=0, concat_axis=0
    )
    biases = jnp.stack(
        [jnp.pad(b, (0, dc - b.shape[0])) for b in (first_bias, second_bias, upper_bias, lower_bias)]
    )
    ids = jnp.stack([row_id, col_id]).astype(jnp.int32)
    bounds = tile_bounds(tile_reach, row_id, col_id, n_row, n_col, tile_rows, tile_cols, own)
    bounds = jnp.broadcast_to(bounds[:, :, None], bounds.shape + (128,))
    early = (ids, bounds, biases, setup_call(first_weight, second_weight))
    moved, early = lax.optimization_barrier((moved, early))
    ids, bounds, biases, taps = early

    rows = moved.transpose(1, 0, 2)
    above, below = halo_rows(rows, n_row * n_col)
    return main_call(
        geom, ids, above + [rows] + below, bounds, *taps, biases, proj_weight,
        upper_weight.reshape(9, dc, dc), lower_weight.reshape(9, dc, dc), chans,
    )


def solution(mesh):
    in_specs = (P("row", "col"), P(), P(), P(), P(), P(), P(), P(), P(), P(), P())
    out_specs = P(("row", "col"), None, None)
    return jax.shard_map(
        on_device, mesh=mesh, in_specs=in_specs, out_specs=out_specs, check_vma=False
    )
```

profile of v0, /device:TPU:4, one launch (start us, length us, event | category | flops | bytes accessed | tf_op | source)
XLA Modules:
  0.0 76.2 jit_solution(13612411391026496531)
XLA Ops:
  0.0 0.0 copy-start
  0.0 1.8 %reshape.270 = bf16[8,4,5120]{2,1,0:T(4,128)(2,1)} reshape(bf16[32,5120]{1,0:T(8,128)(2,1)} %param.11) | data formatting | bytes 655360 | tf_op jit(solution)/shard_map/reshape | solution.py:420
  1.8 4.9 %all-to-all-start = ((bf16[8,4,5120]{2,1,0:T(4,128)(2,1)}), bf16[8,4,5120]{2,1,0:T(4,128)(2,1)S(1)}, u32[]{:S(2)}, u32[]{:S(2)}) async-start(bf16[8,4,5120]{2,1,0:T(4,128)(2,1)} %reshape.270), calls=%async_computation | async-start | bytes 655360 | tf_op jit(solution)/shard_map/all_to_all | solution.py:419
  6.8 0.1 broadcast_in_dim.45
  6.8 0.1 broadcast_in_dim.47
  6.9 0.1 broadcast_multiply_fusion
  7.0 0.1 fusion.2
  7.1 0.0 copy-done
  7.1 0.6 gather_fusion
  7.7 0.1 sub.73
  7.8 0.1 add.70
  7.9 0.1 sub.65
  8.0 0.1 sub.66
  8.0 0.1 broadcast_in_dim.42
  8.1 0.1 broadcast_in_dim.43
  8.2 0.1 add.66
  8.3 0.1 add.67
  8.4 0.7 pad.7
  9.0 0.7 pad.8
  9.7 0.1 squeeze.8
  9.8 0.1 squeeze.9
  9.9 0.0 copy-start.2
  9.9 0.0 copy-start.3
  9.9 4.5 %shard_map.109 = (bf16[3072,256]{1,0:T(8,128)(2,1)}, bf16[1024,256]{1,0:T(8,128)(2,1)}, bf16[3072,256]{1,0:T(8,128)(2,1)}, bf16[1024,256]{1,0:T(8,128)(2,1)}) custom-call(bf16[3,3,320,320]{3,2,1,0:T(8,128)(2,1)} %w1_ref.1, bf16[3,3,320,320]{3,2,1,0:T(8,128)(2,1)} %w2_ref.1), custom_call_target="tpu_custom_call" | custom-call | bytes 8388608 | tf_op jit(solution)/shard_map/pallas_call | solution.py:50
  14.4 0.6 pad_add_fusion.1.refs_0_
  15.0 0.0 copy-done.2
  15.1 0.0 copy-done.3
  15.1 0.6 pad_maximum_fusion.refs_6_
  15.7 2.2 %all-to-all-done = bf16[8,4,5120]{2,1,0:T(4,128)(2,1)S(1)} async-done(((bf16[8,4,5120]{2,1,0:T(4,128)(2,1)}), bf16[8,4,5120]{2,1,0:T(4,128)(2,1)S(1)}, u32[]{:S(2)}, u32[]{:S(2)}) %all-to-all-start) | async-done | bytes 327712 | tf_op jit(solution)/shard_map/all_to_all | solution.py:419
  17.9 0.7 broadcast_in_dim.49.refs_1_
  18.5 0.1 copy.15
  18.6 0.0 copy-start.1
  18.7 4.2 %collective-permute-start.1 = (bf16[3,8,5120]{2,1,0:T(8,128)(2,1)S(1)}, bf16[3,8,5120]{2,1,0:T(8,128)(2,1)S(1)}, u32[]{:S(2)}, u32[]{:S(2)}) collective-permute-start(bf16[3,8,5120]{2,1,0:T(8,128)(2,1)S(1)} %get-tuple-element.35), channel_id=1, source_target_pairs={{1,0},{2,1},{3,2},{4,3},{5,4},{6,5},{7,6},{8,7},{9,8},{10,9},{11,1... | collective-permute-start | bytes 737288 | tf_op jit(solution)/shard_map/ppermute | solution.py:398
  22.9 1.9 %collective-permute-start = (bf16[3,8,5120]{2,1,0:T(8,128)(2,1)S(1)}, bf16[3,8,5120]{2,1,0:T(8,128)(2,1)S(1)}, u32[]{:S(2)}, u32[]{:S(2)}) collective-permute-start(bf16[3,8,5120]{2,1,0:T(8,128)(2,1)S(1)} %get-tuple-element.36), channel_id=1, source_target_pairs={{0,1},{1,2},{2,3},{3,4},{4,5},{5,6},{6,7},{7,8},{8,9},{9,10},{10,1... | collective-permute-start | bytes 737288 | tf_op jit(solution)/shard_map/ppermute | solution.py:397
  24.8 4.3 %collective-permute-done.1.refs_12_ = bf16[3,8,5120]{2,1,0:T(8,128)(2,1)S(1)} collective-permute-done((bf16[3,8,5120]{2,1,0:T(8,128)(2,1)S(1)}, bf16[3,8,5120]{2,1,0:T(8,128)(2,1)S(1)}, u32[]{:S(2)}, u32[]{:S(2)}) %collective-permute-start.1) | collective-permute-done | bytes 245792 | tf_op jit(solution)/shard_map/ppermute | solution.py:398
  29.1 0.0 copy-start.4
  29.1 4.9 %collective-permute-done.refs_10_ = bf16[3,8,5120]{2,1,0:T(8,128)(2,1)S(1)} collective-permute-done((bf16[3,8,5120]{2,1,0:T(8,128)(2,1)S(1)}, bf16[3,8,5120]{2,1,0:T(8,128)(2,1)S(1)}, u32[]{:S(2)}, u32[]{:S(2)}) %collective-permute-start) | collective-permute-done | bytes 245792 | tf_op jit(solution)/shard_map/ppermute | solution.py:397
  34.0 0.0 copy-start.5
  34.0 0.0 copy-done.1
  34.0 0.0 copy-done.4
  34.0 0.7 copy-done.5
  34.7 41.3 %shard_map.110 = bf16[8,256,512]{2,1,0:T(8,128)(2,1)} custom-call(s32[2]{0:T(128)} %pad_add_fusion.1.refs_0_, s32[4,16,128]{2,1,0:T(8,128)} %broadcast_in_dim.49.refs_1_, bf16[3072,256]{1,0:T(8,128)(2,1)} %get-tuple-element.23.refs_2_, bf16[1024,256]{1,0:T(8,128)(2,1)} %get-tuple-element.24.refs_3_, bf16[3072,256]{1,0:T(8,128)(2,1)} %get-tuple-element.25.refs_4_, ...), custom_call_target="tpu_custom_call" | custom-call | flops 24999999488 | bytes 20971520 | tf_op jit(solution)/shard_map/pallas_call | solution.py:352
  (12 shorter events, 0.1 us)
Async XLA Ops:
  0.0 7.1 %copy-start = (s32[4,8,4]{1,2,0:T(4,128)S(1)}, s32[4,8,4]{1,2,0:T(4,128)}, u32[]{:S(2)}) copy-start(s32[4,8,4]{1,2,0:T(4,128)} %param.12) | copy-start | bytes 1540
  1.8 16.0 %all-to-all-start = ((bf16[8,4,5120]{2,1,0:T(4,128)(2,1)}), bf16[8,4,5120]{2,1,0:T(4,128)(2,1)S(1)}, u32[]{:S(2)}, u32[]{:S(2)}) async-start(bf16[8,4,5120]{2,1,0:T(4,128)(2,1)} %reshape.270), calls=%async_computation | async-start | bytes 655360 | tf_op jit(solution)/shard_map/all_to_all | solution.py:419
  9.9 5.2 %copy-start.2 = (f32[512]{0:T(512)S(1)}, f32[512]{0:T(512)}, u32[]{:S(2)}) copy-start(f32[512]{0:T(512)} %param.21) | copy-start | bytes 6148
  9.9 5.2 %copy-start.3 = (f32[512]{0:T(512)S(1)}, f32[512]{0:T(512)}, u32[]{:S(2)}) copy-start(f32[512]{0:T(512)} %param.19) | copy-start | bytes 6148
  18.6 15.3 %copy-start.1 = (bf16[8,4,5120]{2,0,1:T(8,128)(2,1)}, bf16[8,4,5120]{2,0,1:T(8,128)(2,1)S(1)}, u32[]{:S(2)}) copy-start(bf16[8,4,5120]{2,0,1:T(8,128)(2,1)S(1)} %copy.15) | copy-start | bytes 983044
  18.7 10.4 %collective-permute-start.1 = (bf16[3,8,5120]{2,1,0:T(8,128)(2,1)S(1)}, bf16[3,8,5120]{2,1,0:T(8,128)(2,1)S(1)}, u32[]{:S(2)}, u32[]{:S(2)}) collective-permute-start(bf16[3,8,5120]{2,1,0:T(8,128)(2,1)S(1)} %get-tuple-element.35), channel_id=1, source_target_pairs={{1,0},{2,1},{3,2},{4,3},{5,4},{6,5},{7,6},{8,7},{9,8},{10,9},{11,1... | collective-permute-start | bytes 737288 | tf_op jit(solution)/shard_map/ppermute | solution.py:398
  22.9 11.1 %collective-permute-start = (bf16[3,8,5120]{2,1,0:T(8,128)(2,1)S(1)}, bf16[3,8,5120]{2,1,0:T(8,128)(2,1)S(1)}, u32[]{:S(2)}, u32[]{:S(2)}) collective-permute-start(bf16[3,8,5120]{2,1,0:T(8,128)(2,1)S(1)} %get-tuple-element.36), channel_id=1, source_target_pairs={{0,1},{1,2},{2,3},{3,4},{4,5},{5,6},{6,7},{7,8},{8,9},{9,10},{10,1... | collective-permute-start | bytes 737288 | tf_op jit(solution)/shard_map/ppermute | solution.py:397
  29.1 4.9 %copy-start.4 = (bf16[3,8,5120]{2,1,0:T(8,128)(2,1)}, bf16[3,8,5120]{2,1,0:T(8,128)(2,1)S(1)}, u32[]{:S(2)}) copy-start(bf16[3,8,5120]{2,1,0:T(8,128)(2,1)S(1)} %collective-permute-done.1.refs_12_) | copy-start | bytes 737284
  34.0 0.7 copy-start.5
where the time goes:
time: 76.5 us; the launch traced here: 76.2 us
  Pallas kernels  45.8 us (60%)
  waiting for transfers between devices  11.4 us (15%)
  starting transfers between devices  11 us (14%)
  local copies, waits for them, and re-layouts  6.28 us (8%)
  other arithmetic  1.49 us (2%)
    pallas_call x1, Pallas kernels, main_call(): pl.pallas_call(kernel, out_shape=jax.ShapeDtypeStruct((2 * own, 2 * width...  41.3 us
    ppermute x1, waiting for transfers between devices, halo_rows(): lax.ppermute(rows[own - take:], ('row', 'col'), [(i, i + hop) for i in ra...  4.89 us
    all_to_all x1, starting transfers between devices, on_device(): lax.all_to_all(latent.reshape(n_col, own, tile_cols * chans), 'col', spli...  4.88 us
    pallas_call x1, Pallas kernels, setup_call(): pl.pallas_call(setup_kernel, out_shape=taps + taps, compiler_params=pltpu...  4.48 us
    ppermute x1, waiting for transfers between devices, halo_rows(): lax.ppermute(rows[:take], ('row', 'col'), [(i + hop, i) for i in range(n_...  4.29 us
    ppermute x1, starting transfers between devices, halo_rows(): lax.ppermute(rows[:take], ('row', 'col'), [(i + hop, i) for i in range(n_...  4.15 us
    all_to_all x1, waiting for transfers between devices, on_device(): lax.all_to_all(latent.reshape(n_col, own, tile_cols * chans), 'col', spli...  2.19 us
    ppermute x1, starting transfers between devices, halo_rows(): lax.ppermute(rows[own - take:], ('row', 'col'), [(i, i + hop) for i in ra...  1.92 us
  transfers between devices with their start and end apart: 3, of which 3 were waited for; matrix products, arithmetic and copies ran while one was open for 6% of the time, Pallas kernels for 6%

commit v1 on v0

--- a/solution.py
+++ b/solution.py
@@ -10,6 +10,7 @@
 MARGIN = 4
 HALO = 3
 VMEM_LIMIT = 62 * 1024 * 1024
+PAIR_ORDER = ((0, 0), (0, 1), (1, 0), (1, 1), (0, 2), (1, 2), (2, 0), (2, 1), (2, 2))
 
 
 def silu(v):
@@ -66,7 +67,7 @@
     rest_ref[r, :, :, 128:] = after.astype(BF)
 
 
-def conv_group(main_ref, rest_ref, w_main, w_rest, start, rows):
+def conv_group(main_ref, rest_ref, w_main, w_rest, start, rows, tail):
     span, slots = rest_ref.shape[1:3]
     main = main_ref.shape[3]
     size = rows * span * slots
@@ -76,16 +77,20 @@
             parts.append(main_ref[pl.ds(start + dy, rows), pl.ds(dx, span)].reshape(size, main))
         parts.append(rest_ref[pl.ds(start + dy, rows)].reshape(size, 256))
     big = jnp.dot(jnp.concatenate(parts, axis=1), w_main[...], preferred_element_type=F32)
-    size = (rows + 2) * span * slots
-    parts = [main_ref[pl.ds(start, rows + 2), pl.ds(dx, span)].reshape(size, main) for dx in range(3)]
-    parts.append(rest_ref[pl.ds(start, rows + 2)].reshape(size, 256))
+    fresh = start + 2 if tail is not None else start
+    count = rows + 2 - (fresh - start)
+    size = count * span * slots
+    parts = [main_ref[pl.ds(fresh, count), pl.ds(dx, span)].reshape(size, main) for dx in range(3)]
+    parts.append(rest_ref[pl.ds(fresh, count)].reshape(size, 256))
     part = jnp.dot(jnp.concatenate(parts, axis=1), w_rest[...], preferred_element_type=F32)
-    part = part.reshape(rows + 2, span, slots, 256)
+    part = part.reshape(count, span, slots, 256)
+    if tail is not None:
+        part = jnp.concatenate([tail, part], axis=0)
     rest = part[:-2, :, :, :128] + pltpu.roll(part[1:-1, :, :, :128], 64, 3) + part[2:, :, :, 128:]
-    return big.reshape(rows, span, slots, main), rest
-
-
-def tile_body(geom, chans, tall, bounds_ref, m1, r1, b1_ref, m2, r2, b2_ref, canvas, xm, xr, am, ar, cells_ref, beside):
+    return big.reshape(rows, span, slots, main), rest, part[-2:]
+
+
+def tile_body(geom, chans, tall, params, m1, r1, b1_ref, m2, r2, b2_ref, canvas, xm, xr, am, ar, cells_ref, waits):
     n_row, n_col, tile_rows, tile_cols, own = geom
     slots = 2 * n_col
     span = tile_cols + 2 * MARGIN
@@ -95,6 +100,15 @@
     width = n_col * tile_cols
     live = (lax.broadcasted_iota(jnp.int32, (1, 1, 128), 2) < chans - main).astype(F32)
     cell = lax.broadcasted_iota(jnp.int32, (span, slots, 128), 0)
+    slot = lax.broadcasted_iota(jnp.int32, (slots, 128), 0)
+
+    def per_slot(k):
+        out = jnp.zeros((slots, 128), jnp.int32)
+        for i in range(slots):
+            out = jnp.where(slot == i, params[k * slots + i], out)
+        return out
+
+    bounds_ref = [per_slot(k) for k in range(4)]
     cols_ok = ((cell >= bounds_ref[2]) & (cell < bounds_ref[3])).astype(F32)
     xm[...] = jnp.zeros_like(xm)
     am[...] = jnp.zeros_like(am)
@@ -129,19 +143,20 @@
 
     group1 = (rows_x - 2) // 2
     def first(g, carry):
-        beside[0](g)
-        big, rest = conv_group(xm, xr, m1, r1, g * group1, group1)
+        big, rest, tail = conv_group(xm, xr, m1, r1, g * group1, group1, carry)
         for i in range(group1):
             a = g * group1 + i
             v = jnp.concatenate([big[i], rest[i] * live], axis=2) + b1_ref[...]
             put_cells(am, ar, a, silu(v) * wide(mask_of(a + 1)), main)
-        return carry
-    lax.fori_loop(0, 2, first, 0)
+        return tail
+    waits[0]()
+    tail = None
+    for g in range(2):
+        tail = first(g, tail)
 
     group2 = (rows_x - 4) // 2
     def second(g, carry):
-        beside[1](g)
-        big, rest = conv_group(am, ar, m2, r2, g * group2, group2)
+        big, rest, tail = conv_group(am, ar, m2, r2, g * group2, group2, carry)
         for i in range(group2):
             a = g * group2 + i
             v = jnp.concatenate([big[i], rest[i] * live], axis=2) + b2_ref[...]
@@ -167,8 +182,11 @@
             for c in range(tile_cols):
                 for lane in range(lanes // 128):
                     canvas[lane, pl.ds(a * width + c, n_col, stride=tile_cols), :] = blend[c, :, lane * 128 : lane * 128 + 128]
-        return carry
-    lax.fori_loop(0, 2, second, 0)
+        return tail
+    waits[1]()
+    tail = None
+    for g in range(2):
+        tail = second(g, tail)
 
 
 def tile_scratch(geom, chans):
@@ -187,36 +205,44 @@
     ]
 
 
-def phase_part(w, out, k0, kn):
-    ks = pl.ds(k0, kn)
-    depth = w.shape[1]
-    x = [[w[3 * dy + dx, ks, :].astype(F32) for dx in range(3)] for dy in range(3)]
-    rowed = (
-        (x[0], [a + b for a, b in zip(x[1], x[2])]),
-        ([a + b for a, b in zip(x[0], x[1])], x[2]),
-    )
-    for p in range(2):
-        for tap in range(2):
-            u = rowed[p][tap]
-            at = 2 * tap * depth + k0
-            out[0, p, pl.ds(at, kn), :] = u[0].astype(BF)
-            out[0, p, pl.ds(at + depth, kn), :] = (u[1] + u[2]).astype(BF)
-            out[1, p, pl.ds(at, kn), :] = (u[0] + u[1]).astype(BF)
-            out[1, p, pl.ds(at + depth, kn), :] = u[2].astype(BF)
-
-
-def pair_part(w, out, k0, kn):
-    ks = pl.ds(k0, kn)
+def halves(first, second, third):
+    half = 0.5 * second
+    return first + half, third + half, half
+
+
+def weight_kernel(upper_ref, lower_ref, upper_out, pair_out):
+    w = [[upper_ref[3 * dy + dx].astype(F32) for dx in range(3)] for dy in range(3)]
+    rows = [halves(w[0][dx], w[1][dx], w[2][dx]) for dx in range(3)]
+    both = [halves(rows[0][r], rows[1][r], rows[2][r]) for r in range(3)]
+    for i, (r, c) in enumerate(PAIR_ORDER):
+        upper_out[i] = both[r][c].astype(BF)
     for dy in range(3):
-        ends = 0.5 * (w[3 * dy, ks, :].astype(F32) + w[3 * dy + 2, ks, :].astype(F32))
-        mid = 0.5 * w[3 * dy + 1, ks, :].astype(F32)
-        w[3 * dy + 1, ks, :] = (ends + mid).astype(BF)
-        out[dy, ks, :] = (ends - mid).astype(BF)
+        ends = 0.5 * (lower_ref[3 * dy].astype(F32) + lower_ref[3 * dy + 2].astype(F32))
+        mid = 0.5 * lower_ref[3 * dy + 1].astype(F32)
+        pair_out[0, dy] = (ends + mid).astype(BF)
+        pair_out[1, dy] = (ends - mid).astype(BF)
+
+
+def weight_call(upper, lower):
+    dc = upper.shape[2]
+    step = 128
+    return pl.pallas_call(
+        weight_kernel,
+        grid=(dc // step,),
+        out_shape=(jax.ShapeDtypeStruct((9, dc, dc), BF), jax.ShapeDtypeStruct((2, 3, dc, dc), BF)),
+        in_specs=[pl.BlockSpec((9, step, dc), lambda i: (0, i, 0))] * 2,
+        out_specs=(
+            pl.BlockSpec((9, step, dc), lambda i: (0, i, 0)),
+            pl.BlockSpec((2, 3, step, dc), lambda i: (0, 0, i, 0)),
+        ),
+        compiler_params=pltpu.CompilerParams(vmem_limit_bytes=VMEM_LIMIT),
+        cost_estimate=pl.CostEstimate(flops=40 * dc * dc, bytes_accessed=66 * dc * dc, transcendentals=0),
+    )(upper, lower)
 
 
 def decoder_body(
-    keep, canvas, proj_ref, ub_ref, lb_ref, out_ref, left, hid, right, comps, edge, zipped,
-    upper_v, lower_raw, pair_v,
+    keep, canvas, proj_ref, ub_ref, lb_ref, out_hbm, out_ref, out_sems, hid, beyond, across, down, down_beyond,
+    down_across, first, comps, edge, zipped, upper_v, lower_v, waits,
 ):
     rows, width, dc = hid.shape
     steps = rows - 1
@@ -225,120 +251,138 @@
     main = chans // 128 * 128
 
     edge[...] = jnp.zeros_like(edge)
-
-    def hidden_row(r, carry):
-        at = pl.ds(pl.multiple_of(r * width, width), width)
+    first[...] = jnp.zeros_like(first)
+    waits[0]()
+    last = None
+    for r in range(rows):
+        at = pl.ds(r * width, width)
         x = jnp.concatenate([canvas[lane, at, :] for lane in range(main // 128)], axis=1).astype(BF)
         rest = canvas[main // 128, at, :].astype(BF)[:, : chans - main]
         h = jnp.dot(x, proj_ref[:main, :], preferred_element_type=F32)
         h = h + jnp.dot(rest, proj_ref[main:, :], preferred_element_type=F32)
         h = h.astype(BF)
         hid[r] = h
-        edge[0, pl.ds(8, width), :] = h.astype(F32)
-        left[r] = edge[0, pl.ds(7, width), :].astype(BF)
-        right[r] = edge[0, pl.ds(9, width), :].astype(BF)
-        return carry
-
-    lax.fori_loop(0, rows, hidden_row, 0)
-
-    def up_step(p, carry):
-        acts = []
-        for side, srcs in ((0, (left, hid)), (1, (hid, right))):
-            lhs = jnp.concatenate(
-                [src[pl.ds(i, steps)].reshape(steps * width, dc) for i in range(2) for src in srcs], axis=1
-            )
-            v = jnp.dot(lhs, upper_v[side, p], preferred_element_type=F32)
-            acts.append(silu(v + ub_ref[...]).reshape(steps, width, dc))
+        h = h.astype(F32)
+        edge[0, pl.ds(8, width), :] = h
+        first[pl.ds(r, 1), :] = h[:1]
+        b = edge[0, pl.ds(9, width), :]
+        beyond[r] = b.astype(BF)
+        across[r] = (h - b).astype(BF)
+        if last is not None:
+            down[r - 1] = (last[0] - h).astype(BF)
+            down_beyond[r - 1] = (last[1] - b).astype(BF)
+            down_across[r - 1] = ((last[0] - h) - (last[1] - b)).astype(BF)
+        last = (h, b)
+
+    waits[1]()
+    near, far = first[pl.ds(0, 16), :], first[pl.ds(1, 16), :]
+    none = jnp.zeros((16, dc), BF)
+
+    def side(ref, start, extra):
+        return jnp.concatenate([ref[pl.ds(start, steps)].reshape(steps * width, dc), extra.astype(BF)], axis=0)
+
+    def product(parts, at):
+        rhs = upper_v[pl.ds(at, len(parts))].reshape(len(parts) * dc, dc)
+        return jnp.dot(jnp.concatenate(parts, axis=1), rhs, preferred_element_type=F32)
+
+    sums = product([side(hid, 0, none), side(beyond, 0, near), side(hid, 1, none), side(beyond, 1, far)], 0)
+    cols = product([side(across, 0, -near), side(across, 1, -far)], 4)
+    lines = product([side(down, 0, none), side(down_beyond, 0, near - far)], 6)
+    cross = product([side(down_across, 0, far - near)], 8)
+    col_id = lax.broadcasted_iota(jnp.int32, (width, 1), 0)
+    for p in (1, 0):
+        if p == 1:
+            straight, turned = sums + lines, cols + cross
+        else:
+            straight, turned = sums - lines, cols - cross
+        odd = silu(straight + turned + ub_ref[...])
+        even = silu(straight - turned + ub_ref[...])
         for k in range(steps):
             scale = 1.0
-            if k == 0:
-                scale = jnp.where(p == 1, keep[0], 1.0)
-            if k == steps - 1:
-                scale = jnp.where(p == 0, keep[1], 1.0)
-            e = (acts[0][k] * scale).astype(BF).astype(F32)
-            o = (acts[1][k] * scale).astype(BF).astype(F32)
+            if k == 0 and p == 1:
+                scale = keep[0]
+            if k == steps - 1 and p == 0:
+                scale = keep[1]
+            o = (odd[k * width : (k + 1) * width] * scale).astype(BF).astype(F32)
+            after = (even[k * width : (k + 1) * width] * scale).astype(BF).astype(F32)
+            after = jnp.where(col_id < width - 1, after, 0.0)
+            start = (even[steps * width + k : steps * width + k + 1] * scale).astype(BF).astype(F32)
             edge[0, pl.ds(8, width), :] = o
-            edge[1, pl.ds(8, width), :] = e
+            edge[1, pl.ds(8, width), :] = after
+            edge[1, pl.ds(7, 1), :] = start
+            e = edge[1, pl.ds(7, width), :]
             at = 2 * k + 1 - p
             comps[0, at] = (edge[0, pl.ds(7, width), :] - o).astype(BF)
             comps[1, at] = (e + o).astype(BF)
             comps[2, at] = (o - e).astype(BF)
-            comps[3, at] = (e - edge[1, pl.ds(9, width), :]).astype(BF)
-        return carry
-
-    lax.fori_loop(0, 2, up_step, 0)
-
-    group = max(own, 1)
-
-    def low_step(n, carry):
+            comps[3, at] = (e - after).astype(BF)
+
+    waits[2]()
+    group = own
+    copies = []
+    for n in range(2 * own // group):
         start = n * group
         prods = []
         for i in range(4):
-            total = None
-            for dy in range(3):
-                lhs = comps[i, pl.ds(start + dy, group)].reshape(group * width, dc)
-                rhs = pair_v[dy] if i == 2 else lower_raw[3 * dy + (0, 1, 0, 2)[i]]
-                v = jnp.dot(lhs, rhs, preferred_element_type=F32)
-                total = v if total is None else total + v
-            prods.append(total)
-        both = (prods[0] + prods[1] + prods[2], prods[1] - prods[2] - prods[3])
+            lhs = jnp.concatenate(
+                [comps[i, pl.ds(start + dy, group)].reshape(group * width, dc) for dy in range(3)], axis=1)
+            prods.append(jnp.dot(lhs, lower_v[i].reshape(3 * dc, dc), preferred_element_type=F32))
+        both = (prods[0] + (prods[1] + prods[2]), (prods[1] - prods[2]) - prods[3])
         for g in range(group):
-            base = hid[1 + lax.div(start + g, 2)].astype(F32) + lb_ref[...]
-            for side in range(2):
-                v = both[side][g * width : (g + 1) * width] + base
+            base = hid[1 + (start + g) // 2].astype(F32) + lb_ref[...]
+            for q in range(2):
+                v = both[q][g * width : (g + 1) * width] + base
                 for lane in range(dc // 128):
-                    zipped[lane, pl.ds(g * 2 * width + side, width, stride=2), :] = v[:, lane * 128 : lane * 128 + 128]
+                    zipped[lane, pl.ds(g * 2 * width + q, width, stride=2), :] = v[:, lane * 128 : lane * 128 + 128]
             for lane in range(dc // 128):
                 out_ref[start + g, :, pl.ds(lane * 128, 128)] = zipped[lane, pl.ds(g * 2 * width, 2 * width), :].astype(BF)
-        return carry
-
-    lax.fori_loop(0, 2 * own // group, low_step, 0)
-
-
-def main_kernel(
-    geom, chans, n_tall, ids_ref, bounds_ref, m1, r1, m2, r2, bias_ref, proj_ref, upper_ref, lower_ref, *refs
-):
+        copy = pltpu.make_async_copy(out_ref.at[pl.ds(start, group)], out_hbm.at[pl.ds(start, group)], out_sems.at[n])
+        copy.start()
+        copies.append(copy)
+    for copy in copies:
+        copy.wait()
+
+
+def main_kernel(geom, chans, n_tall, params, bias_ref, *refs):
     n_row, n_col, tile_rows, tile_cols, own = geom
-    tall, refs = refs[:n_tall], refs[n_tall:]
-    (out_ref, canvas, xm, xr, am, ar, cells_ref, left, hid, right, comps, edge, zipped,
-     upper_raw, upper_v, lower_raw, pair_v, sems) = refs
-    upper_copy = pltpu.make_async_copy(upper_ref, upper_raw, sems.at[0])
-    lower_copy = pltpu.make_async_copy(lower_ref, lower_raw, sems.at[1])
-    upper_copy.start()
-    lower_copy.start()
-    first_row = ids_ref[0] * tile_rows + ids_ref[1] * own
+    m1_in, r1_in, m2_in, r2_in, proj_in, upper_in, pair_in, lower_in = refs[:8]
+    tall, refs = refs[8 : 8 + n_tall], refs[8 + n_tall :]
+    (out_hbm, canvas, xm, xr, am, ar, cells_ref, hid, beyond, across, down, down_beyond, down_across, first, comps,
+     edge, zipped, out_ref, m1, r1, m2, r2, proj, upper, lower, sems, out_sems) = refs
+    moves = [
+        (m1_in, m1), (r1_in, r1), (m2_in, m2), (r2_in, r2), (proj_in, proj), (upper_in, upper),
+        (pair_in, lower.at[pl.ds(1, 2)]), (lower_in.at[:, 0], lower.at[0]), (lower_in.at[:, 2], lower.at[3]),
+    ]
+    copies = [pltpu.make_async_copy(src, dst, sems.at[i]) for i, (src, dst) in enumerate(moves)]
+    for copy in copies:
+        copy.start()
+
+    def wait_for(*which):
+        def wait():
+            for i in which:
+                copies[i].wait()
+        return wait
+
+    base = 8 * n_col
+    first_row = params[base] * tile_rows + params[base + 1] * own
     keep = (
         jnp.where(first_row > 0, 1.0, 0.0),
         jnp.where(first_row + own < n_row * tile_rows, 1.0, 0.0),
     )
     lanes = chans // 128 * 128 + 128
     bias1, bias2 = bias_ref.at[pl.ds(0, 1), pl.ds(0, lanes)], bias_ref.at[pl.ds(1, 1), pl.ds(0, lanes)]
-    part = upper_raw.shape[1] // 4
-
-    def beside_first(g):
-        @pl.when(g == 0)
-        def _():
-            upper_copy.wait()
-        phase_part(upper_raw, upper_v, pl.multiple_of(g * part, part), part)
-
-    def beside_second(g):
-        @pl.when(g == 0)
-        def _():
-            lower_copy.wait()
-        phase_part(upper_raw, upper_v, pl.multiple_of((g + 2) * part, part), part)
-        pair_part(lower_raw, pair_v, pl.multiple_of(2 * g * part, 2 * part), 2 * part)
-
     tile_body(
-        geom, chans, tall, bounds_ref, m1, r1, bias1, m2, r2, bias2, canvas, xm, xr, am, ar, cells_ref,
-        (beside_first, beside_second),
+        geom, chans, tall, params, m1, r1, bias1, m2, r2, bias2, canvas, xm, xr, am, ar, cells_ref,
+        (wait_for(0, 1), wait_for(2, 3)),
     )
     decoder_body(
-        keep, canvas, proj_ref, bias_ref.at[pl.ds(2, 1)], bias_ref.at[pl.ds(3, 1)], out_ref,
-        left, hid, right, comps, edge, zipped, upper_v, lower_raw, pair_v,
-    )
-
-
-def main_call(geom, ids, tall, bounds, m1, r1, m2, r2, biases, proj, upper, lower, chans):
+        keep, canvas, proj, bias_ref.at[pl.ds(2, 1)], bias_ref.at[pl.ds(3, 1)], out_hbm, out_ref, out_sems,
+        hid, beyond, across, down, down_beyond, down_across, first, comps, edge, zipped, upper, lower,
+        (wait_for(4), wait_for(5), wait_for(6, 7, 8)),
+    )
+
+
+def main_call(geom, params, tall, m1, r1, m2, r2, biases, proj, upper, pair, lower, chans):
     n_row, n_col, tile_rows, tile_cols, own = geom
     width = n_col * tile_cols
     rows = own + 2
@@ -352,25 +396,27 @@
     return pl.pallas_call(
         kernel,
         out_shape=jax.ShapeDtypeStruct((2 * own, 2 * width, dc), BF),
-        in_specs=[pl.BlockSpec(memory_space=pltpu.SMEM)] + [vm] * 7 + [anyspace] * 2 + [vm] * len(tall),
-        out_specs=vm,
+        in_specs=[pl.BlockSpec(memory_space=pltpu.SMEM), vm] + [anyspace] * 8 + [vm] * len(tall),
+        out_specs=anyspace,
         scratch_shapes=tile_scratch(geom, chans)
+        + [pltpu.VMEM((rows, width, dc), BF)] * 3
+        + [pltpu.VMEM((rows - 1, width, dc), BF)] * 3
         + [
-            pltpu.VMEM((rows, width, dc), BF),
-            pltpu.VMEM((rows, width, dc), BF),
-            pltpu.VMEM((rows, width, dc), BF),
+            pltpu.VMEM((24, dc), F32),
             pltpu.VMEM((4, 2 * own + 2, width, dc), BF),
             pltpu.VMEM((2, width + 16, dc), F32),
             pltpu.VMEM((dc // 128, 2 * own * width, 128), F32),
-            pltpu.VMEM(upper.shape, BF),
-            pltpu.VMEM((2, 2, 4 * dc, dc), BF),
-            pltpu.VMEM(lower.shape, BF),
-            pltpu.VMEM((3, dc, dc), BF),
+            pltpu.VMEM((2 * own, 2 * width, dc), BF),
+        ]
+        + [pltpu.VMEM(u.shape, BF) for u in (m1, r1, m2, r2, proj, upper)]
+        + [
+            pltpu.VMEM((4, 3, dc, dc), BF),
+            pltpu.SemaphoreType.DMA((9,)),
             pltpu.SemaphoreType.DMA((2,)),
         ],
         compiler_params=pltpu.CompilerParams(vmem_limit_bytes=VMEM_LIMIT),
         cost_estimate=pl.CostEstimate(flops=25_000_000_000, bytes_accessed=20 << 20, transcendentals=0),
-    )(ids, bounds, m1, r1, m2, r2, biases, proj, upper, lower, *tall)
+    )(params, biases, m1, r1, m2, r2, proj, upper, pair, lower, *tall)
 
 
 def tile_bounds(tile_reach, row_id, col_id, n_row, n_col, tile_rows, tile_cols, own):
@@ -422,18 +468,19 @@
     biases = jnp.stack(
         [jnp.pad(b, (0, dc - b.shape[0])) for b in (first_bias, second_bias, upper_bias, lower_bias)]
     )
-    ids = jnp.stack([row_id, col_id]).astype(jnp.int32)
     bounds = tile_bounds(tile_reach, row_id, col_id, n_row, n_col, tile_rows, tile_cols, own)
-    bounds = jnp.broadcast_to(bounds[:, :, None], bounds.shape + (128,))
-    early = (ids, bounds, biases, setup_call(first_weight, second_weight))
-    moved, early = lax.optimization_barrier((moved, early))
-    ids, bounds, biases, taps = early
+    params = jnp.concatenate([bounds.reshape(-1), jnp.stack([row_id, col_id]).astype(jnp.int32)])
+    early = (params, biases, setup_call(first_weight, second_weight))
+    moved, early, upper_weight, lower_weight = lax.optimization_barrier(
+        (moved, early, upper_weight, lower_weight)
+    )
+    params, biases, taps = early
 
     rows = moved.transpose(1, 0, 2)
     above, below = halo_rows(rows, n_row * n_col)
+    upper, pair = weight_call(upper_weight.reshape(9, dc, dc), lower_weight.reshape(9, dc, dc))
     return main_call(
-        geom, ids, above + [rows] + below, bounds, *taps, biases, proj_weight,
-        upper_weight.reshape(9, dc, dc), lower_weight.reshape(9, dc, dc), chans,
+        geom, params, above + [rows] + below, *taps, biases, proj_weight, upper, pair, lower_weight, chans,
     )
 
 

time: 76.5 us -> 67.6 us (0.88)
  waiting for transfers between devices: 11.4 us -> 4.2 us
  local copies, waits for them, and re-layouts: 6.28 us -> 4.71 us
    pallas_call x1, Pallas kernels: 41.3 us -> 33.3 us  [main_call(): pl.pallas_call(kernel, out_shape=jax.ShapeDtypeStruct((2 * own, 2 * width...]
    pallas_call x0 -> x1, Pallas kernels: none -> 7.96 us  [weight_call(): pl.pallas_call(weight_kernel, grid=(dc // step,), out_shape=(jax.ShapeDty...]
    ppermute x1, waiting for transfers between devices: 4.29 us -> 0.01 us  [halo_rows(): lax.ppermute(rows[:take], ('row', 'col'), [(i + hop, i) for i in range(n_...]
    ppermute x1, waiting for transfers between devices: 4.89 us -> 1.21 us  [halo_rows(): lax.ppermute(rows[own - take:], ('row', 'col'), [(i, i + hop) for i in ra...]
    broadcast_in_dim x7 -> x0, local copies, waits for them, and re-layouts: 1.02 us -> none  [the longest x1 0.68 us: on_device(): bounds = jnp.broadcast_to(bounds[:, :, None], bounds.shape + (128,))]
    all_to_all x1, waiting for transfers between devices: 2.19 us -> 2.99 us  [on_device(): lax.all_to_all(latent.reshape(n_col, own, tile_cols * chans), 'col', spli...]
  transfers between devices with their start and end apart: 3 -> 3, of which waited for: 3 -> 2; matrix products, arithmetic and copies ran while one was open for 6% -> 5% of each run, Pallas kernels for 6% -> 19%
where the time goes in v1:
time: 67.6 us; the launch traced here: 67 us
  Pallas kernels  45.7 us (68%)
  starting transfers between devices  10.5 us (16%)
  local copies, waits for them, and re-layouts  4.71 us (7%)
  waiting for transfers between devices  4.2 us (6%)
  other arithmetic  1.55 us (2%)
    pallas_call x1, Pallas kernels, main_call(): pl.pallas_call(kernel, out_shape=jax.ShapeDtypeStruct((2 * own, 2 * width...  33.3 us
    pallas_call x1, Pallas kernels, weight_call(): pl.pallas_call(weight_kernel, grid=(dc // step,), out_shape=(jax.ShapeDty...  7.96 us
    all_to_all x1, starting transfers between devices, on_device(): lax.all_to_all(latent.reshape(n_col, own, tile_cols * chans), 'col', spli...  4.88 us
    pallas_call x1, Pallas kernels, setup_call(): pl.pallas_call(setup_kernel, out_shape=taps + taps, compiler_params=pltpu...  4.52 us
    ppermute x1, starting transfers between devices, halo_rows(): lax.ppermute(rows[:take], ('row', 'col'), [(i + hop, i) for i in range(n_...  3.71 us
    all_to_all x1, waiting for transfers between devices, on_device(): lax.all_to_all(latent.reshape(n_col, own, tile_cols * chans), 'col', spli...  2.99 us
    ppermute x1, starting transfers between devices, halo_rows(): lax.ppermute(rows[own - take:], ('row', 'col'), [(i, i + hop) for i in ra...  1.92 us
    reshape x1, local copies, waits for them, and re-layouts, on_device(): latent.reshape(n_col, own, tile_cols * chans)  1.83 us
  transfers between devices with their start and end apart: 3, of which 2 were waited for; matrix products, arithmetic and copies ran while one was open for 5% of the time, Pallas kernels for 19%

profile of v1, /device:TPU:4, one launch (start us, length us, event | category | flops | bytes accessed | tf_op | source)
XLA Modules:
  0.0 67.0 jit_solution(4077729112877151593)
XLA Ops:
  0.0 0.0 copy-start
  0.0 1.8 %reshape.295 = bf16[8,4,5120]{2,1,0:T(4,128)(2,1)} reshape(bf16[32,5120]{1,0:T(8,128)(2,1)} %param.11) | data formatting | bytes 655360 | tf_op jit(solution)/shard_map/reshape | solution.py:466
  1.8 4.9 %all-to-all-start = ((bf16[8,4,5120]{2,1,0:T(4,128)(2,1)}), bf16[8,4,5120]{2,1,0:T(4,128)(2,1)S(1)}, u32[]{:S(2)}, u32[]{:S(2)}) async-start(bf16[8,4,5120]{2,1,0:T(4,128)(2,1)} %reshape.295), calls=%async_computation | async-start | bytes 655360 | tf_op jit(solution)/shard_map/all_to_all | solution.py:465
  6.7 0.1 broadcast_multiply_fusion
  6.8 0.1 fusion
  6.9 0.0 copy-done
  6.9 0.6 gather_fusion
  7.5 0.7 %pad.7 = f32[512]{0:T(512)S(1)} pad(f32[320]{0:T(512)} %param.14, f32[]{:T(128)} %constant.10.clone.1), padding=0_192 | pad | bytes 3332 | tf_op jit(solution)/shard_map/jit(_pad)/pad | solution.py:469
  8.2 0.7 %pad.8 = f32[512]{0:T(512)S(1)} pad(f32[320]{0:T(512)} %param.16, f32[]{:T(128)} %constant.10.clone.1), padding=0_192 | pad | bytes 3332 | tf_op jit(solution)/shard_map/jit(_pad)/pad | solution.py:469
  8.9 0.1 subtract_select_fusion
  9.0 0.1 reshape_reshape.3
  9.1 0.0 copy-start.2
  9.1 0.0 copy-start.3
  9.1 4.5 %shard_map.109 = (bf16[3072,256]{1,0:T(8,128)(2,1)}, bf16[1024,256]{1,0:T(8,128)(2,1)}, bf16[3072,256]{1,0:T(8,128)(2,1)}, bf16[1024,256]{1,0:T(8,128)(2,1)}) custom-call(bf16[3,3,320,320]{3,2,1,0:T(8,128)(2,1)} %w1_ref.1, bf16[3,3,320,320]{3,2,1,0:T(8,128)(2,1)} %w2_ref.1), custom_call_target="tpu_custom_call" | custom-call | bytes 8388608 | tf_op jit(solution)/shard_map/pallas_call | solution.py:51
  13.6 0.7 pad_add_fusion.2.refs_0_
  14.3 0.0 copy-done.2
  14.3 0.0 copy-done.3
  14.3 0.6 pad_maximum_fusion.refs_1_
  14.9 3.0 %all-to-all-done = bf16[8,4,5120]{2,1,0:T(4,128)(2,1)S(1)} async-done(((bf16[8,4,5120]{2,1,0:T(4,128)(2,1)}), bf16[8,4,5120]{2,1,0:T(4,128)(2,1)S(1)}, u32[]{:S(2)}, u32[]{:S(2)}) %all-to-all-start) | async-done | bytes 327712 | tf_op jit(solution)/shard_map/all_to_all | solution.py:465
  17.9 0.1 copy.15
  18.0 0.0 copy-start.1
  18.0 3.7 %collective-permute-start.1 = (bf16[3,8,5120]{2,1,0:T(8,128)(2,1)S(1)}, bf16[3,8,5120]{2,1,0:T(8,128)(2,1)S(1)}, u32[]{:S(2)}, u32[]{:S(2)}) collective-permute-start(bf16[3,8,5120]{2,1,0:T(8,128)(2,1)S(1)} %get-tuple-element.37), channel_id=1, source_target_pairs={{1,0},{2,1},{3,2},{4,3},{5,4},{6,5},{7,6},{8,7},{9,8},{10,9},{11,1... | collective-permute-start | bytes 737288 | tf_op jit(solution)/shard_map/ppermute | solution.py:444
  21.7 1.9 %collective-permute-start = (bf16[3,8,5120]{2,1,0:T(8,128)(2,1)S(1)}, bf16[3,8,5120]{2,1,0:T(8,128)(2,1)S(1)}, u32[]{:S(2)}, u32[]{:S(2)}) collective-permute-start(bf16[3,8,5120]{2,1,0:T(8,128)(2,1)S(1)} %get-tuple-element.38), channel_id=1, source_target_pairs={{0,1},{1,2},{2,3},{3,4},{4,5},{5,6},{6,7},{7,8},{8,9},{9,10},{10,1... | collective-permute-start | bytes 737288 | tf_op jit(solution)/shard_map/ppermute | solution.py:443
  23.7 8.0 %shard_map.110 = (bf16[9,512,512]{2,1,0:T(8,128)(2,1)}, bf16[2,3,512,512]{3,2,1,0:T(8,128)(2,1)}) custom-call(bf16[9,512,512]{2,1,0:T(8,128)(2,1)} %bitcast.20, bf16[9,512,512]{2,1,0:T(8,128)(2,1)} %bitcast.21), custom_call_target="tpu_custom_call" | custom-call | flops 10485760 | bytes 17301504 | tf_op jit(solution)/shard_map/pallas_call | solution.py:229
  31.6 0.0 copy-done.1
  31.6 0.0 collective-permute-done.1.refs_12_
  31.6 0.0 copy-start.4
  31.6 1.2 %collective-permute-done.refs_10_ = bf16[3,8,5120]{2,1,0:T(8,128)(2,1)S(1)} collective-permute-done((bf16[3,8,5120]{2,1,0:T(8,128)(2,1)S(1)}, bf16[3,8,5120]{2,1,0:T(8,128)(2,1)S(1)}, u32[]{:S(2)}, u32[]{:S(2)}) %collective-permute-start) | collective-permute-done | bytes 245792 | tf_op jit(solution)/shard_map/ppermute | solution.py:443
  32.8 0.0 copy-start.5
  32.9 0.0 copy-done.4
  32.9 0.7 %copy-done.5 = bf16[3,8,5120]{2,1,0:T(8,128)(2,1)} copy-done((bf16[3,8,5120]{2,1,0:T(8,128)(2,1)}, bf16[3,8,5120]{2,1,0:T(8,128)(2,1)S(1)}, u32[]{:S(2)}) %copy-start.5) | copy-done | bytes 245784
  33.5 33.3 %shard_map.111 = bf16[8,256,512]{2,1,0:T(8,128)(2,1)} custom-call(s32[66]{0:T(128)} %pad_add_fusion.2.refs_0_, f32[4,512]{1,0:T(4,128)} %pad_maximum_fusion.refs_1_, bf16[3072,256]{1,0:T(8,128)(2,1)} %get-tuple-element.26.refs_2_, bf16[1024,256]{1,0:T(8,128)(2,1)} %get-tuple-element.27.refs_3_, bf16[3072,256]{1,0:T(8,128)(2,1)} %get-tuple-element.28.refs_4_, ...), custom_call_target="tpu_custom_call" | custom-call | flops 24999999488 | bytes 20971520 | tf_op jit(solution)/shard_map/pallas_call | solution.py:396
  (9 shorter events, 0.1 us)
Async XLA Ops:
  0.0 6.9 %copy-start = (s32[4,8,4]{1,2,0:T(4,128)S(1)}, s32[4,8,4]{1,2,0:T(4,128)}, u32[]{:S(2)}) copy-start(s32[4,8,4]{1,2,0:T(4,128)} %param.12) | copy-start | bytes 1540
  1.8 16.0 %all-to-all-start = ((bf16[8,4,5120]{2,1,0:T(4,128)(2,1)}), bf16[8,4,5120]{2,1,0:T(4,128)(2,1)S(1)}, u32[]{:S(2)}, u32[]{:S(2)}) async-start(bf16[8,4,5120]{2,1,0:T(4,128)(2,1)} %reshape.295), calls=%async_computation | async-start | bytes 655360 | tf_op jit(solution)/shard_map/all_to_all | solution.py:465
  9.1 5.2 %copy-start.2 = (f32[512]{0:T(512)S(1)}, f32[512]{0:T(512)}, u32[]{:S(2)}) copy-start(f32[512]{0:T(512)} %param.21) | copy-start | bytes 6148
  9.1 5.2 %copy-start.3 = (f32[512]{0:T(512)S(1)}, f32[512]{0:T(512)}, u32[]{:S(2)}) copy-start(f32[512]{0:T(512)} %param.19) | copy-start | bytes 6148
  18.0 13.7 %copy-start.1 = (bf16[8,4,5120]{2,0,1:T(8,128)(2,1)}, bf16[8,4,5120]{2,0,1:T(8,128)(2,1)S(1)}, u32[]{:S(2)}) copy-start(bf16[8,4,5120]{2,0,1:T(8,128)(2,1)S(1)} %copy.15) | copy-start | bytes 983044
  18.0 13.6 %collective-permute-start.1 = (bf16[3,8,5120]{2,1,0:T(8,128)(2,1)S(1)}, bf16[3,8,5120]{2,1,0:T(8,128)(2,1)S(1)}, u32[]{:S(2)}, u32[]{:S(2)}) collective-permute-start(bf16[3,8,5120]{2,1,0:T(8,128)(2,1)S(1)} %get-tuple-element.37), channel_id=1, source_target_pairs={{1,0},{2,1},{3,2},{4,3},{5,4},{6,5},{7,6},{8,7},{9,8},{10,9},{11,1... | collective-permute-start | bytes 737288 | tf_op jit(solution)/shard_map/ppermute | solution.py:444
  21.7 11.1 %collective-permute-start = (bf16[3,8,5120]{2,1,0:T(8,128)(2,1)S(1)}, bf16[3,8,5120]{2,1,0:T(8,128)(2,1)S(1)}, u32[]{:S(2)}, u32[]{:S(2)}) collective-permute-start(bf16[3,8,5120]{2,1,0:T(8,128)(2,1)S(1)} %get-tuple-element.38), channel_id=1, source_target_pairs={{0,1},{1,2},{2,3},{3,4},{4,5},{5,6},{6,7},{7,8},{8,9},{9,10},{10,1... | collective-permute-start | bytes 737288 | tf_op jit(solution)/shard_map/ppermute | solution.py:443
  31.6 1.2 %copy-start.4 = (bf16[3,8,5120]{2,1,0:T(8,128)(2,1)}, bf16[3,8,5120]{2,1,0:T(8,128)(2,1)S(1)}, u32[]{:S(2)}) copy-start(bf16[3,8,5120]{2,1,0:T(8,128)(2,1)S(1)} %collective-permute-done.1.refs_12_) | copy-start | bytes 737284
  32.8 0.7 %copy-start.5 = (bf16[3,8,5120]{2,1,0:T(8,128)(2,1)}, bf16[3,8,5120]{2,1,0:T(8,128)(2,1)S(1)}, u32[]{:S(2)}) copy-start(bf16[3,8,5120]{2,1,0:T(8,128)(2,1)S(1)} %collective-permute-done.refs_10_) | copy-start | bytes 737284

commit v2 on v1

--- a/solution.py
+++ b/solution.py
@@ -122,13 +122,17 @@
         return jnp.concatenate([m] * (lanes // 128), axis=2)
 
     r = 0
-    for piece in tall:
-        for k in range(piece.shape[0]):
+    is_odd = lax.rem(params[4 * slots + 1], 2) == 1
+    for on_odd, on_even in tall:
+        for k in range(on_odd.shape[0]):
             cols = []
             for c in range(tile_cols):
                 lo = c * chans
                 off = lo % 128
-                v = piece[k, :, lo - off : lo - off + lanes].astype(F32)
+                at = slice(lo - off, lo - off + lanes)
+                v = on_odd[k, :, at].astype(F32)
+                if on_even is not on_odd:
+                    v = jnp.where(is_odd, v, on_even[k, :, at].astype(F32))
                 if off:
                     v = pltpu.roll(v, lanes - off, 1)
                 cols.append(v)
@@ -156,6 +160,7 @@
 
     group2 = (rows_x - 4) // 2
     def second(g, carry):
+        waits[2](g)
         big, rest, tail = conv_group(am, ar, m2, r2, g * group2, group2, carry)
         for i in range(group2):
             a = g * group2 + i
@@ -210,34 +215,45 @@
     return first + half, third + half, half
 
 
-def weight_kernel(upper_ref, lower_ref, upper_out, pair_out):
-    w = [[upper_ref[3 * dy + dx].astype(F32) for dx in range(3)] for dy in range(3)]
-    rows = [halves(w[0][dx], w[1][dx], w[2][dx]) for dx in range(3)]
-    both = [halves(rows[0][r], rows[1][r], rows[2][r]) for r in range(3)]
-    for i, (r, c) in enumerate(PAIR_ORDER):
-        upper_out[i] = both[r][c].astype(BF)
+def upper_kernel(w_hbm, out_hbm, w_ref, out_ref, in_sems, out_sems):
+    step = w_ref.shape[1] // 4
+    parts = [pl.ds(i * step, step) for i in range(4)]
+    reads = [pltpu.make_async_copy(w_hbm.at[:, at], w_ref.at[:, at], in_sems.at[i]) for i, at in enumerate(parts)]
+    writes = [pltpu.make_async_copy(out_ref.at[:, at], out_hbm.at[:, at], out_sems.at[i]) for i, at in enumerate(parts)]
+    for read in reads:
+        read.start()
+    for read, write, at in zip(reads, writes, parts):
+        read.wait()
+        w = [[w_ref[3 * dy + dx, at, :].astype(F32) for dx in range(3)] for dy in range(3)]
+        rows = [halves(w[0][dx], w[1][dx], w[2][dx]) for dx in range(3)]
+        both = [halves(rows[0][r], rows[1][r], rows[2][r]) for r in range(3)]
+        for i, (r, c) in enumerate(PAIR_ORDER):
+            out_ref[i, at, :] = both[r][c].astype(BF)
+        write.start()
+    for write in writes:
+        write.wait()
+
+
+def upper_call(w):
+    anyspace = pl.BlockSpec(memory_space=pl.ANY)
+    return pl.pallas_call(
+        upper_kernel,
+        out_shape=jax.ShapeDtypeStruct(w.shape, BF),
+        in_specs=[anyspace],
+        out_specs=anyspace,
+        scratch_shapes=[pltpu.VMEM(w.shape, BF)] * 2 + [pltpu.SemaphoreType.DMA((4,))] * 2,
+        compiler_params=pltpu.CompilerParams(vmem_limit_bytes=VMEM_LIMIT),
+        cost_estimate=pl.CostEstimate(flops=0, bytes_accessed=4 * w.size, transcendentals=0),
+    )(w)
+
+
+def pair_part(w, k0, kn):
+    ks = pl.ds(k0, kn)
     for dy in range(3):
-        ends = 0.5 * (lower_ref[3 * dy].astype(F32) + lower_ref[3 * dy + 2].astype(F32))
-        mid = 0.5 * lower_ref[3 * dy + 1].astype(F32)
-        pair_out[0, dy] = (ends + mid).astype(BF)
-        pair_out[1, dy] = (ends - mid).astype(BF)
-
-
-def weight_call(upper, lower):
-    dc = upper.shape[2]
-    step = 128
-    return pl.pallas_call(
-        weight_kernel,
-        grid=(dc // step,),
-        out_shape=(jax.ShapeDtypeStruct((9, dc, dc), BF), jax.ShapeDtypeStruct((2, 3, dc, dc), BF)),
-        in_specs=[pl.BlockSpec((9, step, dc), lambda i: (0, i, 0))] * 2,
-        out_specs=(
-            pl.BlockSpec((9, step, dc), lambda i: (0, i, 0)),
-            pl.BlockSpec((2, 3, step, dc), lambda i: (0, 0, i, 0)),
-        ),
-        compiler_params=pltpu.CompilerParams(vmem_limit_bytes=VMEM_LIMIT),
-        cost_estimate=pl.CostEstimate(flops=40 * dc * dc, bytes_accessed=66 * dc * dc, transcendentals=0),
-    )(upper, lower)
+        ends = 0.5 * (w[0, dy, ks, :].astype(F32) + w[3, dy, ks, :].astype(F32))
+        mid = 0.5 * w[1, dy, ks, :].astype(F32)
+        w[1, dy, ks, :] = (ends + mid).astype(BF)
+        w[2, dy, ks, :] = (ends - mid).astype(BF)
 
 
 def decoder_body(
@@ -317,7 +333,6 @@
             comps[2, at] = (o - e).astype(BF)
             comps[3, at] = (e - after).astype(BF)
 
-    waits[2]()
     group = own
     copies = []
     for n in range(2 * own // group):
@@ -343,15 +358,17 @@
         copy.wait()
 
 
-def main_kernel(geom, chans, n_tall, params, bias_ref, *refs):
+def main_kernel(geom, chans, pick, params, bias_ref, *refs):
     n_row, n_col, tile_rows, tile_cols, own = geom
-    m1_in, r1_in, m2_in, r2_in, proj_in, upper_in, pair_in, lower_in = refs[:8]
-    tall, refs = refs[8 : 8 + n_tall], refs[8 + n_tall :]
+    m1_in, r1_in, m2_in, r2_in, proj_in, upper_in, lower_in = refs[:7]
+    n_tall = 1 + max(max(p) for p in pick)
+    tall = [(refs[7 + a], refs[7 + b]) for a, b in pick]
+    refs = refs[7 + n_tall :]
     (out_hbm, canvas, xm, xr, am, ar, cells_ref, hid, beyond, across, down, down_beyond, down_across, first, comps,
      edge, zipped, out_ref, m1, r1, m2, r2, proj, upper, lower, sems, out_sems) = refs
     moves = [
         (m1_in, m1), (r1_in, r1), (m2_in, m2), (r2_in, r2), (proj_in, proj), (upper_in, upper),
-        (pair_in, lower.at[pl.ds(1, 2)]), (lower_in.at[:, 0], lower.at[0]), (lower_in.at[:, 2], lower.at[3]),
+        (lower_in.at[:, 0], lower.at[0]), (lower_in.at[:, 1], lower.at[1]), (lower_in.at[:, 2], lower.at[3]),
     ]
     copies = [pltpu.make_async_copy(src, dst, sems.at[i]) for i, (src, dst) in enumerate(moves)]
     for copy in copies:
@@ -370,19 +387,27 @@
         jnp.where(first_row + own < n_row * tile_rows, 1.0, 0.0),
     )
     lanes = chans // 128 * 128 + 128
-    bias1, bias2 = bias_ref.at[pl.ds(0, 1), pl.ds(0, lanes)], bias_ref.at[pl.ds(1, 1), pl.ds(0, lanes)]
+    bias1, bias2 = bias_ref.at[:, pl.ds(0, lanes)], bias_ref.at[:, pl.ds(lanes, lanes)]
+    dc = proj.shape[1]
+    part = dc // 2
+
+    def beside(g):
+        if g == 0:
+            wait_for(6, 7, 8)()
+        pair_part(lower, g * part, part)
+
     tile_body(
         geom, chans, tall, params, m1, r1, bias1, m2, r2, bias2, canvas, xm, xr, am, ar, cells_ref,
-        (wait_for(0, 1), wait_for(2, 3)),
+        (wait_for(0, 1), wait_for(2, 3), beside),
     )
     decoder_body(
-        keep, canvas, proj, bias_ref.at[pl.ds(2, 1)], bias_ref.at[pl.ds(3, 1)], out_hbm, out_ref, out_sems,
+        keep, canvas, proj, bias_ref.at[:, pl.ds(2 * lanes, dc)], bias_ref.at[:, pl.ds(2 * lanes + dc, dc)], out_hbm, out_ref, out_sems,
         hid, beyond, across, down, down_beyond, down_across, first, comps, edge, zipped, upper, lower,
-        (wait_for(4), wait_for(5), wait_for(6, 7, 8)),
+        (wait_for(4), wait_for(5)),
     )
 
 
-def main_call(geom, params, tall, m1, r1, m2, r2, biases, proj, upper, pair, lower, chans):
+def main_call(geom, params, tall, pick, m1, r1, m2, r2, biases, proj, upper, lower, chans):
     n_row, n_col, tile_rows, tile_cols, own = geom
     width = n_col * tile_cols
     rows = own + 2
@@ -391,12 +416,12 @@
     anyspace = pl.BlockSpec(memory_space=pl.ANY)
 
     def kernel(*refs):
-        main_kernel(geom, chans, len(tall), *refs)
+        main_kernel(geom, chans, pick, *refs)
 
     return pl.pallas_call(
         kernel,
         out_shape=jax.ShapeDtypeStruct((2 * own, 2 * width, dc), BF),
-        in_specs=[pl.BlockSpec(memory_space=pltpu.SMEM), vm] + [anyspace] * 8 + [vm] * len(tall),
+        in_specs=[pl.BlockSpec(memory_space=pltpu.SMEM), vm] + [anyspace] * 7 + [vm] * len(tall),
         out_specs=anyspace,
         scratch_shapes=tile_scratch(geom, chans)
         + [pltpu.VMEM((rows, width, dc), BF)] * 3
@@ -416,7 +441,7 @@
         ],
         compiler_params=pltpu.CompilerParams(vmem_limit_bytes=VMEM_LIMIT),
         cost_estimate=pl.CostEstimate(flops=25_000_000_000, bytes_accessed=20 << 20, transcendentals=0),
-    )(params, biases, m1, r1, m2, r2, proj, upper, pair, lower, *tall)
+    )(params, biases, m1, r1, m2, r2, proj, upper, lower, *tall)
 
 
 def tile_bounds(tile_reach, row_id, col_id, n_row, n_col, tile_rows, tile_cols, own):
@@ -432,6 +457,18 @@
     col_lo = jnp.where(tiles > 0, MARGIN - reach[:, :, 2], MARGIN)
     col_hi = jnp.where(tiles < n_col - 1, MARGIN + tile_cols + reach[:, :, 3], MARGIN + tile_cols)
     return jnp.stack([row_lo, row_hi, col_lo, col_hi]).reshape(4, 2 * n_col).astype(jnp.int32)
+
+
+def swapped_rows(rows, odd, n_all):
+    own = rows.shape[0]
+    last = own - HALO
+    between = [(i, i + 1) for i in range(1, n_all - 1, 2)]
+    within = [(i, i + 1) for i in range(0, n_all, 2)]
+    got = []
+    for pairs, start in ((between, jnp.where(odd, last, 0)), (within, jnp.where(odd, 0, last))):
+        part = lax.dynamic_slice_in_dim(rows, start, HALO, axis=0)
+        got.append(lax.ppermute(part, ("row", "col"), pairs + [(b, a) for a, b in pairs]))
+    return got
 
 
 def halo_rows(rows, n_all):
@@ -465,22 +502,25 @@
     moved = lax.all_to_all(
         latent.reshape(n_col, own, tile_cols * chans), "col", split_axis=0, concat_axis=0
     )
-    biases = jnp.stack(
-        [jnp.pad(b, (0, dc - b.shape[0])) for b in (first_bias, second_bias, upper_bias, lower_bias)]
-    )
+    fill = jnp.zeros((-chans % 128,), F32)
+    biases = jnp.concatenate([first_bias, fill, second_bias, fill, upper_bias, lower_bias]).reshape(1, -1)
     bounds = tile_bounds(tile_reach, row_id, col_id, n_row, n_col, tile_rows, tile_cols, own)
     params = jnp.concatenate([bounds.reshape(-1), jnp.stack([row_id, col_id]).astype(jnp.int32)])
     early = (params, biases, setup_call(first_weight, second_weight))
-    moved, early, upper_weight, lower_weight = lax.optimization_barrier(
-        (moved, early, upper_weight, lower_weight)
-    )
+    moved, early, upper_weight = lax.optimization_barrier((moved, early, upper_weight))
     params, biases, taps = early
 
     rows = moved.transpose(1, 0, 2)
-    above, below = halo_rows(rows, n_row * n_col)
-    upper, pair = weight_call(upper_weight.reshape(9, dc, dc), lower_weight.reshape(9, dc, dc))
+    if own >= HALO and n_col % 2 == 0:
+        across, inside = swapped_rows(rows, lax.rem(col_id, 2) == 1, n_row * n_col)
+        tall, pick = [rows, across, inside], [(2, 1), (0, 0), (1, 2)]
+    else:
+        above, below = halo_rows(rows, n_row * n_col)
+        tall = above + [rows] + below
+        pick = [(i, i) for i in range(len(tall))]
+    upper = upper_call(upper_weight.reshape(9, dc, dc))
     return main_call(
-        geom, params, above + [rows] + below, *taps, biases, proj_weight, upper, pair, lower_weight, chans,
+        geom, params, tall, pick, *taps, biases, proj_weight, upper, lower_weight, chans,
     )
 
 

time: 67.6 us -> 64 us (0.947)
  Pallas kernels: 45.7 us -> 41.4 us
  waiting for transfers between devices: 4.2 us -> 6.9 us
  starting transfers between devices: 10.5 us -> 9.08 us
    pallas_call x1, Pallas kernels: 7.96 us -> 3.83 us  [upper_call(): pl.pallas_call(upper_kernel, out_shape=jax.ShapeDtypeStruct(w.shape, BF),...]
    ppermute x2, waiting for transfers between devices: 1.21 us -> 3.22 us  [swapped_rows(): lax.ppermute(part, ('row', 'col'), pairs + [(b, a) for a, b in pairs])]
    ppermute x2, starting transfers between devices: 5.63 us -> 4.2 us  [swapped_rows(): lax.ppermute(part, ('row', 'col'), pairs + [(b, a) for a, b in pairs])]
    pad x2 -> x0, local copies, waits for them, and re-layouts: 1.37 us -> none  [on_device(): jnp.pad(b, (0, dc - b.shape[0]))]
    concatenate x0 -> x1, local copies, waits for them, and re-layouts: none -> 0.81 us  [on_device(): jnp.concatenate([first_bias, fill, second_bias, fill, upper_bias, lower_b...]
    all_to_all x1, waiting for transfers between devices: 2.99 us -> 3.68 us  [on_device(): lax.all_to_all(latent.reshape(n_col, own, tile_cols * chans), 'col', spli...]
  transfers between devices with their start and end apart: 3 -> 3, of which waited for: 2 -> 2; matrix products, arithmetic and copies ran while one was open for 5% -> 5% of each run, Pallas kernels for 19% -> 13%
where the time goes in v2:
time: 64 us; the launch traced here: 63.3 us
  Pallas kernels  41.4 us (65%)
  starting transfers between devices  9.08 us (14%)
  waiting for transfers between devices  6.9 us (11%)
  local copies, waits for them, and re-layouts  4.76 us (7%)
  other arithmetic  0.88 us (1%)
    pallas_call x1, Pallas kernels, main_call(): pl.pallas_call(kernel, out_shape=jax.ShapeDtypeStruct((2 * own, 2 * width...  33.1 us
    all_to_all x1, starting transfers between devices, on_device(): lax.all_to_all(latent.reshape(n_col, own, tile_cols * chans), 'col', spli...  4.88 us
    pallas_call x1, Pallas kernels, setup_call(): pl.pallas_call(setup_kernel, out_shape=taps + taps, compiler_params=pltpu...  4.46 us
    ppermute x2, starting transfers between devices, swapped_rows(): lax.ppermute(part, ('row', 'col'), pairs + [(b, a) for a, b in pairs])  4.2 us
    pallas_call x1, Pallas kernels, upper_call(): pl.pallas_call(upper_kernel, out_shape=jax.ShapeDtypeStruct(w.shape, BF),...  3.83 us
    all_to_all x1, waiting for transfers between devices, on_device(): lax.all_to_all(latent.reshape(n_col, own, tile_cols * chans), 'col', spli...  3.68 us
    ppermute x2, waiting for transfers between devices, swapped_rows(): lax.ppermute(part, ('row', 'col'), pairs + [(b, a) for a, b in pairs])  3.22 us
    reshape x1, local copies, waits for them, and re-layouts, on_device(): latent.reshape(n_col, own, tile_cols * chans)  1.83 us
  transfers between devices with their start and end apart: 3, of which 2 were waited for; matrix products, arithmetic and copies ran while one was open for 5% of the time, Pallas kernels for 13%

profile of v2, /device:TPU:4, one launch (start us, length us, event | category | flops | bytes accessed | tf_op | source)
XLA Modules:
  0.0 63.3 jit_solution(2299542002775720732)
XLA Ops:
  0.0 0.0 copy-start
  0.0 1.8 %reshape.295 = bf16[8,4,5120]{2,1,0:T(4,128)(2,1)} reshape(bf16[32,5120]{1,0:T(8,128)(2,1)} %param.11) | data formatting | bytes 655360 | tf_op jit(solution)/shard_map/reshape | solution.py:503
  1.8 4.9 %all-to-all-start = ((bf16[8,4,5120]{2,1,0:T(4,128)(2,1)}), bf16[8,4,5120]{2,1,0:T(4,128)(2,1)S(1)}, u32[]{:S(2)}, u32[]{:S(2)}) async-start(bf16[8,4,5120]{2,1,0:T(4,128)(2,1)} %reshape.295), calls=%async_computation | async-start | bytes 655360 | tf_op jit(solution)/shard_map/all_to_all | solution.py:502
  6.7 0.1 broadcast_multiply_fusion
  6.8 0.1 fusion
  6.9 0.0 copy-done
  6.9 0.6 gather_fusion
  7.5 0.1 subtract_select_fusion
  7.6 0.1 reshape_reshape.3
  7.7 0.8 %concatenate.29 = f32[1792]{0:T(1024)S(1)} concatenate(f32[320]{0:T(512)} %param.14, f32[64]{0:T(128)S(1)} %broadcast_in_dim.35, f32[320]{0:T(512)} %param.16, f32[64]{0:T(128)S(1)} %broadcast_in_dim.35, f32[512]{0:T(512)} %param.19, f32[512]{0:T(512)} %param.21), dimensions={0} | concatenate | bytes 14336 | tf_op jit(solution)/shard_map/concatenate | solution.py:506
  8.5 0.6 reshape.296.refs_1_
  9.1 4.5 %shard_map.109 = (bf16[3072,256]{1,0:T(8,128)(2,1)}, bf16[1024,256]{1,0:T(8,128)(2,1)}, bf16[3072,256]{1,0:T(8,128)(2,1)}, bf16[1024,256]{1,0:T(8,128)(2,1)}) custom-call(bf16[3,3,320,320]{3,2,1,0:T(8,128)(2,1)} %w1_ref.1, bf16[3,3,320,320]{3,2,1,0:T(8,128)(2,1)} %w2_ref.1), custom_call_target="tpu_custom_call" | custom-call | bytes 8388608 | tf_op jit(solution)/shard_map/pallas_call | solution.py:51
  13.6 0.6 pad_add_fusion.2.refs_0_
  14.2 3.7 %all-to-all-done = bf16[8,4,5120]{2,1,0:T(4,128)(2,1)S(1)} async-done(((bf16[8,4,5120]{2,1,0:T(4,128)(2,1)}), bf16[8,4,5120]{2,1,0:T(4,128)(2,1)S(1)}, u32[]{:S(2)}, u32[]{:S(2)}) %all-to-all-start) | async-done | bytes 327712 | tf_op jit(solution)/shard_map/all_to_all | solution.py:502
  17.9 0.1 copy.18
  18.0 0.0 copy-start.1
  18.0 0.1 collective-permute-start.1
  18.1 4.1 %collective-permute-start = (bf16[3,8,5120]{2,1,0:T(8,128)(2,1)S(1)}, bf16[3,8,5120]{2,1,0:T(8,128)(2,1)S(1)}, u32[]{:S(2)}, u32[]{:S(2)}) collective-permute-start(bf16[3,8,5120]{2,1,0:T(8,128)(2,1)S(1)} %get-tuple-element.32), channel_id=1, source_target_pairs={{1,2},{3,4},{5,6},{7,8},{9,10},{11,12},{13,14},{15,16},{17,18},{19... | collective-permute-start | bytes 737288 | tf_op jit(solution)/shard_map/ppermute | solution.py:470
  22.2 3.8 %shard_map.110.refs_7_ = bf16[9,512,512]{2,1,0:T(8,128)(2,1)} custom-call(bf16[9,512,512]{2,1,0:T(8,128)(2,1)} %bitcast.18), custom_call_target="tpu_custom_call" | custom-call | bytes 9437184 | tf_op jit(solution)/shard_map/pallas_call | solution.py:239
  26.1 0.0 copy-done.1
  26.1 0.0 collective-permute-done.1.refs_11_
  26.1 0.0 copy-start.2
  26.1 3.2 %collective-permute-done.refs_10_ = bf16[3,8,5120]{2,1,0:T(8,128)(2,1)S(1)} collective-permute-done((bf16[3,8,5120]{2,1,0:T(8,128)(2,1)S(1)}, bf16[3,8,5120]{2,1,0:T(8,128)(2,1)S(1)}, u32[]{:S(2)}, u32[]{:S(2)}) %collective-permute-start) | collective-permute-done | bytes 245792 | tf_op jit(solution)/shard_map/ppermute | solution.py:470
  29.3 0.0 copy-start.3
  29.3 0.0 copy-done.2
  29.3 0.7 %copy-done.3 = bf16[3,8,5120]{2,1,0:T(8,128)(2,1)} copy-done((bf16[3,8,5120]{2,1,0:T(8,128)(2,1)}, bf16[3,8,5120]{2,1,0:T(8,128)(2,1)S(1)}, u32[]{:S(2)}) %copy-start.3) | copy-done | bytes 245784
  30.0 33.1 %shard_map.111 = bf16[8,256,512]{2,1,0:T(8,128)(2,1)} custom-call(s32[66]{0:T(128)} %pad_add_fusion.2.refs_0_, f32[1,1792]{1,0:T(1,128)} %reshape.296.refs_1_, bf16[3072,256]{1,0:T(8,128)(2,1)} %get-tuple-element.23.refs_2_, bf16[1024,256]{1,0:T(8,128)(2,1)} %get-tuple-element.24.refs_3_, bf16[3072,256]{1,0:T(8,128)(2,1)} %get-tuple-element.25.refs_4_, ...), custom_call_target="tpu_custom_call" | custom-call | flops 24999999488 | bytes 20971520 | tf_op jit(solution)/shard_map/pallas_call | solution.py:421
  (10 shorter events, 0.1 us)
Async XLA Ops:
  0.0 6.9 %copy-start = (s32[4,8,4]{1,2,0:T(4,128)S(1)}, s32[4,8,4]{1,2,0:T(4,128)}, u32[]{:S(2)}) copy-start(s32[4,8,4]{1,2,0:T(4,128)} %param.12) | copy-start | bytes 1540
  1.8 16.0 %all-to-all-start = ((bf16[8,4,5120]{2,1,0:T(4,128)(2,1)}), bf16[8,4,5120]{2,1,0:T(4,128)(2,1)S(1)}, u32[]{:S(2)}, u32[]{:S(2)}) async-start(bf16[8,4,5120]{2,1,0:T(4,128)(2,1)} %reshape.295), calls=%async_computation | async-start | bytes 655360 | tf_op jit(solution)/shard_map/all_to_all | solution.py:502
  18.0 8.1 %copy-start.1 = (bf16[8,4,5120]{2,0,1:T(8,128)(2,1)}, bf16[8,4,5120]{2,0,1:T(8,128)(2,1)S(1)}, u32[]{:S(2)}) copy-start(bf16[8,4,5120]{2,0,1:T(8,128)(2,1)S(1)} %copy.18) | copy-start | bytes 983044
  18.0 8.1 %collective-permute-start.1 = (bf16[3,8,5120]{2,1,0:T(8,128)(2,1)S(1)}, bf16[3,8,5120]{2,1,0:T(8,128)(2,1)S(1)}, u32[]{:S(2)}, u32[]{:S(2)}) collective-permute-start(bf16[3,8,5120]{2,1,0:T(8,128)(2,1)S(1)} %get-tuple-element.31), channel_id=1, source_target_pairs={{0,1},{2,3},{4,5},{6,7},{8,9},{10,11},{12,13},{14,15},{16,17},{18,... | collective-permute-start | bytes 737288 | tf_op jit(solution)/shard_map/ppermute | solution.py:470
  18.1 11.2 %collective-permute-start = (bf16[3,8,5120]{2,1,0:T(8,128)(2,1)S(1)}, bf16[3,8,5120]{2,1,0:T(8,128)(2,1)S(1)}, u32[]{:S(2)}, u32[]{:S(2)}) collective-permute-start(bf16[3,8,5120]{2,1,0:T(8,128)(2,1)S(1)} %get-tuple-element.32), channel_id=1, source_target_pairs={{1,2},{3,4},{5,6},{7,8},{9,10},{11,12},{13,14},{15,16},{17,18},{19... | collective-permute-start | bytes 737288 | tf_op jit(solution)/shard_map/ppermute | solution.py:470
  26.1 3.2 %copy-start.2 = (bf16[3,8,5120]{2,1,0:T(8,128)(2,1)}, bf16[3,8,5120]{2,1,0:T(8,128)(2,1)S(1)}, u32[]{:S(2)}) copy-start(bf16[3,8,5120]{2,1,0:T(8,128)(2,1)S(1)} %collective-permute-done.1.refs_11_) | copy-start | bytes 737284
  29.3 0.7 %copy-start.3 = (bf16[3,8,5120]{2,1,0:T(8,128)(2,1)}, bf16[3,8,5120]{2,1,0:T(8,128)(2,1)S(1)}, u32[]{:S(2)}) copy-start(bf16[3,8,5120]{2,1,0:T(8,128)(2,1)S(1)} %collective-permute-done.refs_10_) | copy-start | bytes 737284

commit v3 on v2

--- a/solution.py
+++ b/solution.py
@@ -90,7 +90,7 @@
     return big.reshape(rows, span, slots, main), rest, part[-2:]
 
 
-def tile_body(geom, chans, tall, params, m1, r1, b1_ref, m2, r2, b2_ref, canvas, xm, xr, am, ar, cells_ref, waits):
+def tile_body(geom, chans, tall, params, m1, r1, b1_ref, m2, r2, b2_ref, canvas, xm, xr, am, ar, waits):
     n_row, n_col, tile_rows, tile_cols, own = geom
     slots = 2 * n_col
     span = tile_cols + 2 * MARGIN
@@ -136,8 +136,7 @@
                 if off:
                     v = pltpu.roll(v, lanes - off, 1)
                 cols.append(v)
-            cells_ref[...] = jnp.stack(cols, axis=0)
-            v = cells_ref[...]
+            v = jnp.stack(cols, axis=0)
             v = jnp.concatenate([v[:, :, :main], v[:, :, main:] * live], axis=2)
             v = jnp.concatenate(
                 [pltpu.roll(v[-MARGIN:], 1, 1), v, pltpu.roll(v[:MARGIN], n_col - 1, 1)], axis=0)
@@ -206,7 +205,6 @@
         pltpu.VMEM((rows_x, span, slots, 256), BF),
         pltpu.VMEM((rows_x - 2, span + 2, slots, main), BF),
         pltpu.VMEM((rows_x - 2, span, slots, 256), BF),
-        pltpu.VMEM((tile_cols, n_col, main + 128), F32),
     ]
 
 
@@ -351,9 +349,9 @@
                     zipped[lane, pl.ds(g * 2 * width + q, width, stride=2), :] = v[:, lane * 128 : lane * 128 + 128]
             for lane in range(dc // 128):
                 out_ref[start + g, :, pl.ds(lane * 128, 128)] = zipped[lane, pl.ds(g * 2 * width, 2 * width), :].astype(BF)
-        copy = pltpu.make_async_copy(out_ref.at[pl.ds(start, group)], out_hbm.at[pl.ds(start, group)], out_sems.at[n])
-        copy.start()
-        copies.append(copy)
+            copy = pltpu.make_async_copy(out_ref.at[start + g], out_hbm.at[start + g], out_sems.at[start + g])
+            copy.start()
+            copies.append(copy)
     for copy in copies:
         copy.wait()
 
@@ -364,7 +362,7 @@
     n_tall = 1 + max(max(p) for p in pick)
     tall = [(refs[7 + a], refs[7 + b]) for a, b in pick]
     refs = refs[7 + n_tall :]
-    (out_hbm, canvas, xm, xr, am, ar, cells_ref, hid, beyond, across, down, down_beyond, down_across, first, comps,
+    (out_hbm, canvas, xm, xr, am, ar, hid, beyond, across, down, down_beyond, down_across, first, comps,
      edge, zipped, out_ref, m1, r1, m2, r2, proj, upper, lower, sems, out_sems) = refs
     moves = [
         (m1_in, m1), (r1_in, r1), (m2_in, m2), (r2_in, r2), (proj_in, proj), (upper_in, upper),
@@ -397,7 +395,7 @@
         pair_part(lower, g * part, part)
 
     tile_body(
-        geom, chans, tall, params, m1, r1, bias1, m2, r2, bias2, canvas, xm, xr, am, ar, cells_ref,
+        geom, chans, tall, params, m1, r1, bias1, m2, r2, bias2, canvas, xm, xr, am, ar,
         (wait_for(0, 1), wait_for(2, 3), beside),
     )
     decoder_body(
@@ -437,7 +435,7 @@
         + [
             pltpu.VMEM((4, 3, dc, dc), BF),
             pltpu.SemaphoreType.DMA((9,)),
-            pltpu.SemaphoreType.DMA((2,)),
+            pltpu.SemaphoreType.DMA((2 * own,)),
         ],
         compiler_params=pltpu.CompilerParams(vmem_limit_bytes=VMEM_LIMIT),
         cost_estimate=pl.CostEstimate(flops=25_000_000_000, bytes_accessed=20 << 20, transcendentals=0),

time: 64 us -> 63.9 us (level)
  no operation moved by 1% of the time
where the time goes in v3:
time: 63.9 us; the launch traced here: 63.2 us
  Pallas kernels  41.3 us (65%)
  starting transfers between devices  9.08 us (14%)
  waiting for transfers between devices  6.9 us (11%)
  local copies, waits for them, and re-layouts  4.76 us (7%)
  other arithmetic  0.88 us (1%)
    pallas_call x1, Pallas kernels, main_call(): pl.pallas_call(kernel, out_shape=jax.ShapeDtypeStruct((2 * own, 2 * width...  33 us
    all_to_all x1, starting transfers between devices, on_device(): lax.all_to_all(latent.reshape(n_col, own, tile_cols * chans), 'col', spli...  4.88 us
    pallas_call x1, Pallas kernels, setup_call(): pl.pallas_call(setup_kernel, out_shape=taps + taps, compiler_params=pltpu...  4.46 us
    ppermute x2, starting transfers between devices, swapped_rows(): lax.ppermute(part, ('row', 'col'), pairs + [(b, a) for a, b in pairs])  4.2 us
    pallas_call x1, Pallas kernels, upper_call(): pl.pallas_call(upper_kernel, out_shape=jax.ShapeDtypeStruct(w.shape, BF),...  3.83 us
    all_to_all x1, waiting for transfers between devices, on_device(): lax.all_to_all(latent.reshape(n_col, own, tile_cols * chans), 'col', spli...  3.68 us
    ppermute x2, waiting for transfers between devices, swapped_rows(): lax.ppermute(part, ('row', 'col'), pairs + [(b, a) for a, b in pairs])  3.22 us
    reshape x1, local copies, waits for them, and re-layouts, on_device(): latent.reshape(n_col, own, tile_cols * chans)  1.83 us
  transfers between devices with their start and end apart: 3, of which 2 were waited for; matrix products, arithmetic and copies ran while one was open for 5% of the time, Pallas kernels for 13%

profile of v3, /device:TPU:4, one launch (start us, length us, event | category | flops | bytes accessed | tf_op | source)
XLA Modules:
  0.0 63.2 jit_solution(2841708299397665596)
XLA Ops:
  0.0 0.0 copy-start
  0.0 1.8 %reshape.295 = bf16[8,4,5120]{2,1,0:T(4,128)(2,1)} reshape(bf16[32,5120]{1,0:T(8,128)(2,1)} %param.11) | data formatting | bytes 655360 | tf_op jit(solution)/shard_map/reshape | solution.py:501
  1.8 4.9 %all-to-all-start = ((bf16[8,4,5120]{2,1,0:T(4,128)(2,1)}), bf16[8,4,5120]{2,1,0:T(4,128)(2,1)S(1)}, u32[]{:S(2)}, u32[]{:S(2)}) async-start(bf16[8,4,5120]{2,1,0:T(4,128)(2,1)} %reshape.295), calls=%async_computation | async-start | bytes 655360 | tf_op jit(solution)/shard_map/all_to_all | solution.py:500
  6.7 0.1 broadcast_multiply_fusion
  6.8 0.1 fusion
  6.9 0.0 copy-done
  6.9 0.6 gather_fusion
  7.5 0.1 subtract_select_fusion
  7.6 0.1 reshape_reshape.3
  7.7 0.8 %concatenate.29 = f32[1792]{0:T(1024)S(1)} concatenate(f32[320]{0:T(512)} %param.14, f32[64]{0:T(128)S(1)} %broadcast_in_dim.35, f32[320]{0:T(512)} %param.16, f32[64]{0:T(128)S(1)} %broadcast_in_dim.35, f32[512]{0:T(512)} %param.19, f32[512]{0:T(512)} %param.21), dimensions={0} | concatenate | bytes 14336 | tf_op jit(solution)/shard_map/concatenate | solution.py:504
  8.5 0.6 reshape.296.refs_1_
  9.1 4.5 %shard_map.109 = (bf16[3072,256]{1,0:T(8,128)(2,1)}, bf16[1024,256]{1,0:T(8,128)(2,1)}, bf16[3072,256]{1,0:T(8,128)(2,1)}, bf16[1024,256]{1,0:T(8,128)(2,1)}) custom-call(bf16[3,3,320,320]{3,2,1,0:T(8,128)(2,1)} %w1_ref.1, bf16[3,3,320,320]{3,2,1,0:T(8,128)(2,1)} %w2_ref.1), custom_call_target="tpu_custom_call" | custom-call | bytes 8388608 | tf_op jit(solution)/shard_map/pallas_call | solution.py:51
  13.6 0.6 pad_add_fusion.2.refs_0_
  14.2 3.7 %all-to-all-done = bf16[8,4,5120]{2,1,0:T(4,128)(2,1)S(1)} async-done(((bf16[8,4,5120]{2,1,0:T(4,128)(2,1)}), bf16[8,4,5120]{2,1,0:T(4,128)(2,1)S(1)}, u32[]{:S(2)}, u32[]{:S(2)}) %all-to-all-start) | async-done | bytes 327712 | tf_op jit(solution)/shard_map/all_to_all | solution.py:500
  17.9 0.1 copy.18
  18.0 0.0 copy-start.1
  18.0 0.1 collective-permute-start.1
  18.1 4.1 %collective-permute-start = (bf16[3,8,5120]{2,1,0:T(8,128)(2,1)S(1)}, bf16[3,8,5120]{2,1,0:T(8,128)(2,1)S(1)}, u32[]{:S(2)}, u32[]{:S(2)}) collective-permute-start(bf16[3,8,5120]{2,1,0:T(8,128)(2,1)S(1)} %get-tuple-element.32), channel_id=1, source_target_pairs={{1,2},{3,4},{5,6},{7,8},{9,10},{11,12},{13,14},{15,16},{17,18},{19... | collective-permute-start | bytes 737288 | tf_op jit(solution)/shard_map/ppermute | solution.py:468
  22.2 3.8 %shard_map.110.refs_7_ = bf16[9,512,512]{2,1,0:T(8,128)(2,1)} custom-call(bf16[9,512,512]{2,1,0:T(8,128)(2,1)} %bitcast.18), custom_call_target="tpu_custom_call" | custom-call | bytes 9437184 | tf_op jit(solution)/shard_map/pallas_call | solution.py:237
  26.1 0.0 copy-done.1
  26.1 0.0 collective-permute-done.1.refs_11_
  26.1 0.0 copy-start.2
  26.1 3.2 %collective-permute-done.refs_10_ = bf16[3,8,5120]{2,1,0:T(8,128)(2,1)S(1)} collective-permute-done((bf16[3,8,5120]{2,1,0:T(8,128)(2,1)S(1)}, bf16[3,8,5120]{2,1,0:T(8,128)(2,1)S(1)}, u32[]{:S(2)}, u32[]{:S(2)}) %collective-permute-start) | collective-permute-done | bytes 245792 | tf_op jit(solution)/shard_map/ppermute | solution.py:468
  29.3 0.0 copy-start.3
  29.3 0.0 copy-done.2
  29.3 0.7 %copy-done.3 = bf16[3,8,5120]{2,1,0:T(8,128)(2,1)} copy-done((bf16[3,8,5120]{2,1,0:T(8,128)(2,1)}, bf16[3,8,5120]{2,1,0:T(8,128)(2,1)S(1)}, u32[]{:S(2)}) %copy-start.3) | copy-done | bytes 245784
  30.0 33.0 %shard_map.111 = bf16[8,256,512]{2,1,0:T(8,128)(2,1)} custom-call(s32[66]{0:T(128)} %pad_add_fusion.2.refs_0_, f32[1,1792]{1,0:T(1,128)} %reshape.296.refs_1_, bf16[3072,256]{1,0:T(8,128)(2,1)} %get-tuple-element.23.refs_2_, bf16[1024,256]{1,0:T(8,128)(2,1)} %get-tuple-element.24.refs_3_, bf16[3072,256]{1,0:T(8,128)(2,1)} %get-tuple-element.25.refs_4_, ...), custom_call_target="tpu_custom_call" | custom-call | flops 24999999488 | bytes 20971520 | tf_op jit(solution)/shard_map/pallas_call | solution.py:419
  (10 shorter events, 0.1 us)
Async XLA Ops:
  0.0 6.9 %copy-start = (s32[4,8,4]{1,2,0:T(4,128)S(1)}, s32[4,8,4]{1,2,0:T(4,128)}, u32[]{:S(2)}) copy-start(s32[4,8,4]{1,2,0:T(4,128)} %param.12) | copy-start | bytes 1540
  1.8 16.0 %all-to-all-start = ((bf16[8,4,5120]{2,1,0:T(4,128)(2,1)}), bf16[8,4,5120]{2,1,0:T(4,128)(2,1)S(1)}, u32[]{:S(2)}, u32[]{:S(2)}) async-start(bf16[8,4,5120]{2,1,0:T(4,128)(2,1)} %reshape.295), calls=%async_computation | async-start | bytes 655360 | tf_op jit(solution)/shard_map/all_to_all | solution.py:500
  18.0 8.1 %copy-start.1 = (bf16[8,4,5120]{2,0,1:T(8,128)(2,1)}, bf16[8,4,5120]{2,0,1:T(8,128)(2,1)S(1)}, u32[]{:S(2)}) copy-start(bf16[8,4,5120]{2,0,1:T(8,128)(2,1)S(1)} %copy.18) | copy-start | bytes 983044
  18.0 8.1 %collective-permute-start.1 = (bf16[3,8,5120]{2,1,0:T(8,128)(2,1)S(1)}, bf16[3,8,5120]{2,1,0:T(8,128)(2,1)S(1)}, u32[]{:S(2)}, u32[]{:S(2)}) collective-permute-start(bf16[3,8,5120]{2,1,0:T(8,128)(2,1)S(1)} %get-tuple-element.31), channel_id=1, source_target_pairs={{0,1},{2,3},{4,5},{6,7},{8,9},{10,11},{12,13},{14,15},{16,17},{18,... | collective-permute-start | bytes 737288 | tf_op jit(solution)/shard_map/ppermute | solution.py:468
  18.1 11.2 %collective-permute-start = (bf16[3,8,5120]{2,1,0:T(8,128)(2,1)S(1)}, bf16[3,8,5120]{2,1,0:T(8,128)(2,1)S(1)}, u32[]{:S(2)}, u32[]{:S(2)}) collective-permute-start(bf16[3,8,5120]{2,1,0:T(8,128)(2,1)S(1)} %get-tuple-element.32), channel_id=1, source_target_pairs={{1,2},{3,4},{5,6},{7,8},{9,10},{11,12},{13,14},{15,16},{17,18},{19... | collective-permute-start | bytes 737288 | tf_op jit(solution)/shard_map/ppermute | solution.py:468
  26.1 3.2 %copy-start.2 = (bf16[3,8,5120]{2,1,0:T(8,128)(2,1)}, bf16[3,8,5120]{2,1,0:T(8,128)(2,1)S(1)}, u32[]{:S(2)}) copy-start(bf16[3,8,5120]{2,1,0:T(8,128)(2,1)S(1)} %collective-permute-done.1.refs_11_) | copy-start | bytes 737284
  29.3 0.7 %copy-start.3 = (bf16[3,8,5120]{2,1,0:T(8,128)(2,1)}, bf16[3,8,5120]{2,1,0:T(8,128)(2,1)S(1)}, u32[]{:S(2)}) copy-start(bf16[3,8,5120]{2,1,0:T(8,128)(2,1)S(1)} %collective-permute-done.refs_10_) | copy-start | bytes 737284
